TPU v7x, 32 devices: a whole 2x2x4 slice. The times are simulated.
32 devices in a mesh: dp: 4 (over y, core), seq: 8 (over z, x).
Axes of the slice: x: 2, y: 2, z: 4, core: 2. Of those that a mesh axis runs over, the one named last changes fastest.
Arguments:
- inputs: bfloat16 [4, 32768, 768], P('dp', 'seq'), may hold values from -6 to 6
- cotangent: bfloat16 [4, 32768, 768], P('dp', 'seq'), may hold values from -6 to 6
- first_factor: bfloat16 [256, 128, 256], P('dp', 'seq'), may hold values from -0.375 to 0.375
- second_factor: bfloat16 [128, 256, 128], P('dp', 'seq'), may hold values from -0.5 to 0.5
Outputs:
- grad_input: bfloat16 [4, 32768, 768], P('dp', 'seq')
- first_grad: float32 [256, 128, 256], P('dp', 'seq')
- latter_matrix_derivative: float32 [128, 256, 128], P('dp', 'seq')
All inputs are finite; a program needn't handle non-finite values.
Results may differ from a plain program's by a relative error of at most 0.0085.
Values may be sent and summed in bfloat16 or wider, within the bound.
No kernel may reach another device: no remote copies, remote signals or barrier semaphores. Data moves between devices by JAX's collectives and lax.ppermute only.
A program may use at most 128 MiB of HBM per device.

v0:
```python
import jax
import jax.numpy as jnp
from jax import lax
from jax.sharding import PartitionSpec as P


def silu_slope(values):
    logistic = jax.nn.sigmoid(values)
    return logistic * (1.0 + values * (1.0 - logistic))


def body(inputs, cotangent, first_factor, second_factor):
    sequences, tok_rows, channels = inputs.shape
    row_block, local_blocks, size_one = first_factor.shape
    batch_total = sequences * lax.axis_size("dp")
    mean_weight = 1.0 / batch_total
    tile_lattice = inputs.reshape(sequences, local_blocks, size_one, channels)
    line_combined_result = jnp.einsum(
        "ibk,sbkd->sbid",
        lax.all_gather(first_factor, "dp", axis=0, tiled=True),
        tile_lattice,
        preferred_element_type=jnp.float32,
    ).astype(jnp.bfloat16)
    second_full = lax.all_gather(second_factor, "dp", axis=0, tiled=True)
    columns = lax.all_to_all(line_combined_result, "seq", split_axis=2, concat_axis=1, tiled=True)
    product = jnp.einsum(
        "ijk,skjd->sijd", second_full, columns, preferred_element_type=jnp.float32
    ).astype(jnp.bfloat16)
    columns, output = (
        columns,
        lax.all_to_all(product, "seq", split_axis=1, concat_axis=2, tiled=True),
    )
    output = output.reshape(sequences, tok_rows, channels)
    input_wide = inputs.astype(jnp.float32)
    cot_wide = cotangent.astype(jnp.float32)
    upstream = (cot_wide * jax.nn.silu(input_wide)).astype(jnp.bfloat16)
    gate_term = (cot_wide * output.astype(jnp.float32) * silu_slope(input_wide)).astype(
        jnp.bfloat16
    )
    upstream_rows = upstream.reshape(sequences, local_blocks, size_one, channels)
    backward_derivative_columns_local = lax.all_to_all(
        upstream_rows, "seq", split_axis=2, concat_axis=1, tiled=True
    )
    back_cols = jnp.einsum(
        "ijk,sijd->skjd",
        second_full,
        backward_derivative_columns_local,
        preferred_element_type=jnp.float32,
    ).astype(jnp.bfloat16)
    mixed_grad = lax.all_to_all(back_cols, "seq", split_axis=1, concat_axis=2, tiled=True)
    sliced = backward_derivative_columns_local
    latter_matrix_derivative = lax.psum_scatter(
        jnp.einsum("sijd,skjd->ijk", sliced, columns, preferred_element_type=jnp.float32)
        * mean_weight,
        "dp",
        scatter_dimension=0,
        tiled=True,
    )
    sliced = mixed_grad
    first_grad = lax.psum_scatter(
        jnp.einsum("sbid,sbkd->ibk", sliced, tile_lattice, preferred_element_type=jnp.float32)
        * mean_weight,
        "dp",
        scatter_dimension=0,
        tiled=True,
    )
    sliced = mixed_grad
    block_folded = jnp.einsum(
        "ibk,sbid->sbkd",
        lax.all_gather(first_factor, "dp", axis=0, tiled=True),
        sliced,
        preferred_element_type=jnp.float32,
    )
    grad_input = (
        block_folded.reshape(sequences, tok_rows, channels) + gate_term.astype(jnp.float32)
    ).astype(jnp.bfloat16)
    return (grad_input, first_grad, latter_matrix_derivative)


def solution(mesh):
    placed = (
        P("dp", "seq", None),
        P("dp", "seq", None),
        P("dp", "seq", None),
        P("dp", "seq", None),
    )
    return jax.shard_map(
        body,
        mesh=mesh,
        in_specs=placed,
        out_specs=(P("dp", "seq", None), P("dp", "seq", None), P("dp", "seq", None)),
        check_vma=False,
    )
```

profile of v0, /device:TPU:20, one launch (start us, length us, event | category | flops | bytes accessed | tf_op | source)
XLA Modules:
  0.0 633.0 jit_solution(8025054083942597754)
XLA Ops:
  7.2 7.1 %fusion = bf16[1,4096,768]{2,1,0:T(8,128)(2,1)S(1)} fusion(bf16[1,4096,768]{2,1,0:T(8,128)(2,1)} %param.5, bf16[1,4096,768]{2,1,0:T(8,128)(2,1)} %param.4), kind=kLoop, calls=%fused_computation.5 | loop fusion | flops 25165824 | bytes 18874368 | tf_op jit(solution)/shard_map/convert_element_type | solution.py:36
  14.2 6.3 copy.48
  20.5 6.3 all-to-all-start
  27.8 24.6 %all-gather.5.cloned.1.call-done = bf16[256,16,256]{2,0,1:T(8,128)(2,1)} async-done(((bf16[64,16,256]{2,0,1:T(8,128)(2,1)}), bf16[256,16,256]{2,0,1:T(8,128)(2,1)}) %all-gather.5.cloned.1.call-update) | async-done | bytes 2097168 | tf_op jit(solution)/shard_map/all_gather | solution.py:70
  52.3 8.0 %convert_bitcast_fusion.2 = bf16[1,16,256,768]{2,3,1,0:T(8,128)(2,1)} fusion(bf16[16,256,768]{2,1,0:T(8,128)(2,1)} %bitcast.56, bf16[256,16,256]{2,0,1:T(8,128)(2,1)} %all-gather.5.cloned.1.call-done), kind=kOutput, calls=%fused_computation.17 | convolution fusion | flops 1613758464 | bytes 14680064 | tf_op jit(solution)/shard_map/ibk,sbkd->sbid/dot_general | solution.py:18
  60.3 9.0 %copy.57 = bf16[1,16,256,768]{3,1,0,2:T(8,128)(2,1)} copy(bf16[1,16,256,768]{2,3,1,0:T(8,128)(2,1)} %convert_bitcast_fusion.2) | data formatting | bytes 12582912 | tf_op jit(solution)/shard_map/convert_element_type | solution.py:23
  69.3 92.3 %all-to-all-done = bf16[1,16,256,768]{3,1,0,2:T(8,128)(2,1)} async-done(((bf16[1,16,256,768]{3,1,0,2:T(8,128)(2,1)}), bf16[1,16,256,768]{3,1,0,2:T(8,128)(2,1)}, u32[]{:S(2)}, u32[]{:S(2)}) %all-to-all-start) | async-done | bytes 6291488 | tf_op jit(solution)/shard_map/all_to_all | solution.py:41
  161.6 8.1 %all-to-all-start.2 = ((bf16[1,16,256,768]{3,1,0,2:T(8,128)(2,1)}), bf16[1,16,256,768]{3,1,0,2:T(8,128)(2,1)}, u32[]{:S(2)}, u32[]{:S(2)}) async-start(bf16[1,16,256,768]{3,1,0,2:T(8,128)(2,1)} %copy.57), calls=%async_computation.2 | async-start | bytes 12582912 | tf_op jit(solution)/shard_map/all_to_all | solution.py:25
  170.7 4.9 copy.49
  175.6 3.2 copy.50
  178.8 10.6 %all-gather.3.cloned.1.call-done = bf16[128,32,128]{2,0,1:T(8,128)(2,1)} async-done(((bf16[32,32,128]{2,0,1:T(8,128)(2,1)}), bf16[128,32,128]{2,0,1:T(8,128)(2,1)}) %all-gather.3.cloned.1.call-update) | async-done | bytes 1048592 | tf_op jit(solution)/shard_map/all_gather | solution.py:24
  189.4 12.8 %convert_bitcast_fusion.3 = bf16[1,128,32,768]{1,3,2,0:T(8,128)(2,1)} fusion(bf16[128,32,128]{2,0,1:T(8,128)(2,1)} %all-gather.3.cloned.1.call-done, bf16[128,32,768]{2,1,0:T(8,128)(2,1)} %bitcast.64), kind=kOutput, calls=%fused_computation.18 | convolution fusion | flops 808452096 | bytes 13631488 | tf_op jit(solution)/shard_map/ijk,sijd->skjd/dot_general | solution.py:44
  202.2 9.0 %copy.53 = bf16[1,128,32,768]{3,2,0,1:T(8,128)(2,1)} copy(bf16[1,128,32,768]{1,3,2,0:T(8,128)(2,1)} %convert_bitcast_fusion.3) | data formatting | bytes 12582912 | tf_op jit(solution)/shard_map/convert_element_type | solution.py:49
  211.2 92.4 %all-to-all-done.2 = bf16[1,16,256,768]{3,1,0,2:T(8,128)(2,1)} async-done(((bf16[1,16,256,768]{3,1,0,2:T(8,128)(2,1)}), bf16[1,16,256,768]{3,1,0,2:T(8,128)(2,1)}, u32[]{:S(2)}, u32[]{:S(2)}) %all-to-all-start.2) | async-done | bytes 6291488 | tf_op jit(solution)/shard_map/all_to_all | solution.py:25
  303.7 8.3 %all-to-all-start.1 = ((bf16[1,128,32,768]{3,2,0,1:T(8,128)(2,1)}), bf16[1,128,32,768]{3,2,0,1:T(8,128)(2,1)}, u32[]{:S(2)}, u32[]{:S(2)}) async-start(bf16[1,128,32,768]{3,2,0,1:T(8,128)(2,1)} %copy.53), calls=%async_computation.1 | async-start | bytes 12582912 | tf_op jit(solution)/shard_map/all_to_all | solution.py:50
  312.0 4.9 copy.58
  317.5 2.6 copy-done.1
  320.2 9.7 %convert_bitcast_fusion.1 = bf16[1,128,32,768]{1,3,2,0:T(8,128)(2,1)} fusion(bf16[128,32,128]{2,0,1:T(8,128)(2,1)S(1)} %copy-done.3, bf16[128,32,768]{2,1,0:T(8,128)(2,1)S(1)} %bitcast.66), kind=kOutput, calls=%fused_computation.16 | convolution fusion | flops 808452096 | bytes 13631488 | tf_op jit(solution)/shard_map/ijk,skjd->sijd/dot_general | solution.py:26
  329.9 9.1 %copy.61 = bf16[1,128,32,768]{3,2,0,1:T(8,128)(2,1)} copy(bf16[1,128,32,768]{1,3,2,0:T(8,128)(2,1)} %convert_bitcast_fusion.1) | data formatting | bytes 12582912 | tf_op jit(solution)/shard_map/convert_element_type | solution.py:28
  339.0 106.9 %all-to-all-done.1 = bf16[1,128,32,768]{3,2,0,1:T(8,128)(2,1)} async-done(((bf16[1,128,32,768]{3,2,0,1:T(8,128)(2,1)}), bf16[1,128,32,768]{3,2,0,1:T(8,128)(2,1)}, u32[]{:S(2)}, u32[]{:S(2)}) %all-to-all-start.1) | async-done | bytes 6291488 | tf_op jit(solution)/shard_map/all_to_all | solution.py:50
  445.9 8.1 %all-to-all-start.3 = ((bf16[1,128,32,768]{3,2,0,1:T(8,128)(2,1)}), bf16[1,128,32,768]{3,2,0,1:T(8,128)(2,1)}, u32[]{:S(2)}, u32[]{:S(2)}) async-start(bf16[1,128,32,768]{3,2,0,1:T(8,128)(2,1)} %copy.61), calls=%async_computation.3 | async-start | bytes 12582912 | tf_op jit(solution)/shard_map/all_to_all | solution.py:31
  454.0 3.3 copy.54
  457.3 2.7 copy-done
  460.0 6.7 %multiply_bitcast_fusion = f32[256,16,256]{2,0,1:T(8,128)} fusion(bf16[16,256,768]{2,1,0:T(8,128)(2,1)S(1)} %bitcast.60, bf16[16,256,768]{2,1,0:T(8,128)(2,1)} %bitcast.57), kind=kOutput, calls=%fused_computation.26 | convolution fusion | flops 1611661312 | bytes 16777216 | tf_op jit(solution)/shard_map/sbid,sbkd->ibk/dot_general | solution.py:61
  467.0 12.7 %multiply_bitcast_fusion.1 = f32[128,32,128]{0,2,1:T(8,128)} fusion(bf16[128,32,768]{2,1,0:T(8,128)(2,1)} %bitcast.65, bf16[128,32,768]{2,1,0:T(8,128)(2,1)} %bitcast.67), kind=kOutput, calls=%fused_computation.27 | convolution fusion | flops 805830656 | bytes 14680064 | tf_op jit(solution)/shard_map/sijd,skjd->ijk/dot_general | solution.py:53
  479.8 3.5 copy.66
  483.3 9.1 %fusion.24 = f32[16,768,256]{1,2,0:T(8,128)} fusion(bf16[16,256,768]{2,1,0:T(8,128)(2,1)} %bitcast.61, bf16[256,16,256]{2,0,1:T(8,128)(2,1)S(1)} %copy-done.2), kind=kOutput, calls=%fused_computation.28 | convolution fusion | flops 1610612736 | bytes 20971520 | tf_op jit(solution)/shard_map/ibk,sbid->sbkd/dot_general | solution.py:68
  492.4 95.5 %all-to-all-done.3 = bf16[1,128,32,768]{3,2,0,1:T(8,128)(2,1)} async-done(((bf16[1,128,32,768]{3,2,0,1:T(8,128)(2,1)}), bf16[1,128,32,768]{3,2,0,1:T(8,128)(2,1)}, u32[]{:S(2)}, u32[]{:S(2)}) %all-to-all-start.3) | async-done | bytes 6291488 | tf_op jit(solution)/shard_map/all_to_all | solution.py:31
  587.9 9.1 %convert_bitcast_fusion = f32[1,16,8,32,768]{4,3,1,2,0:T(8,128)} fusion(bf16[1,8,16,32,768]{4,3,2,1,0:T(8,128)(2,1)} %bitcast.34), kind=kLoop, calls=%fused_computation.13 | loop fusion | flops 3145728 | bytes 18874368 | tf_op jit(solution)/shard_map/convert_element_type | solution.py:37
  597.1 11.0 %copy.63 = f32[1,16,8,32,768]{4,3,2,1,0:T(8,128)} copy(f32[1,16,8,32,768]{4,3,1,2,0:T(8,128)} %convert_bitcast_fusion) | data formatting | bytes 25165824 | tf_op jit(solution)/shard_map/convert_element_type | solution.py:37
  608.0 15.1 %fusion.8 = bf16[1,4096,768]{2,1,0:T(8,128)(2,1)} fusion(f32[16,768,256]{1,2,0:T(8,128)} %fusion.24, bf16[1,4096,768]{2,1,0:T(8,128)(2,1)S(1)} %bitcast.59, f32[1,16,8,32,768]{4,3,2,1,0:T(8,128)} %copy.63, bf16[1,4096,768]{2,1,0:T(8,128)(2,1)} %param.5), kind=kLoop, calls=%fused_computation.15 | loop fusion | flops 47185920 | bytes 44040192 | tf_op jit(solution)/shard_map/convert_element_type | solution.py:76
  623.1 2.8 copy.67
  (28 shorter events, 2.9 us)
Async XLA Ops:
  20.5 6.3 copy-start.4
  20.5 141.1 %all-to-all-start = ((bf16[1,16,256,768]{3,1,0,2:T(8,128)(2,1)}), bf16[1,16,256,768]{3,1,0,2:T(8,128)(2,1)}, u32[]{:S(2)}, u32[]{:S(2)}) async-start(bf16[1,16,256,768]{3,1,0,2:T(8,128)(2,1)} %copy.48), calls=%async_computation | async-start | bytes 12582912 | tf_op jit(solution)/shard_map/all_to_all | solution.py:41
  26.8 25.5 %all-gather.5.cloned.1.call-start = ((), (), s32[]{:S(2)}) async-start(), calls=%async_computation.7 | async-start | bytes 2621440 | tf_op jit(solution)/shard_map/all_gather | solution.py:70
  69.3 100.6 %copy-start.5 = (bf16[32,32,128]{2,1,0:T(8,128)(2,1)S(1)}, bf16[32,32,128]{2,1,0:T(8,128)(2,1)}, u32[]{:S(2)}) copy-start(bf16[32,32,128]{2,1,0:T(8,128)(2,1)} %param.7) | copy-start | bytes 786436
  161.6 142.1 %all-to-all-start.2 = ((bf16[1,16,256,768]{3,1,0,2:T(8,128)(2,1)}), bf16[1,16,256,768]{3,1,0,2:T(8,128)(2,1)}, u32[]{:S(2)}, u32[]{:S(2)}) async-start(bf16[1,16,256,768]{3,1,0,2:T(8,128)(2,1)} %copy.57), calls=%async_computation.2 | async-start | bytes 12582912 | tf_op jit(solution)/shard_map/all_to_all | solution.py:25
  169.7 19.7 %all-gather.3.cloned.1.call-start = ((), (), s32[]{:S(2)}) async-start(), calls=%async_computation.6 | async-start | bytes 1310720 | tf_op jit(solution)/shard_map/all_gather | solution.py:24
  303.7 142.2 %all-to-all-start.1 = ((bf16[1,128,32,768]{3,2,0,1:T(8,128)(2,1)}), bf16[1,128,32,768]{3,2,0,1:T(8,128)(2,1)}, u32[]{:S(2)}, u32[]{:S(2)}) async-start(bf16[1,128,32,768]{3,2,0,1:T(8,128)(2,1)} %copy.53), calls=%async_computation.1 | async-start | bytes 12582912 | tf_op jit(solution)/shard_map/all_to_all | solution.py:50
  316.9 3.3 copy-start.3
  317.5 2.6 copy-start.1
  445.9 142.0 %all-to-all-start.3 = ((bf16[1,128,32,768]{3,2,0,1:T(8,128)(2,1)}), bf16[1,128,32,768]{3,2,0,1:T(8,128)(2,1)}, u32[]{:S(2)}, u32[]{:S(2)}) async-start(bf16[1,128,32,768]{3,2,0,1:T(8,128)(2,1)} %copy.61), calls=%async_computation.3 | async-start | bytes 12582912 | tf_op jit(solution)/shard_map/all_to_all | solution.py:31
  454.0 169.2 %reduce-scatter.3.cloned.1.call-start = ((), (), s32[]{:S(2)}) async-start(), calls=%async_computation.8 | async-start | bytes 5242880 | tf_op jit(solution)/shard_map/reduce_scatter | solution.py:60
  457.3 2.7 copy-start
  466.7 159.2 %reduce-scatter.5.cloned.1.call-start = ((), (), s32[]{:S(2)}) async-start(), calls=%async_computation.9 | async-start | bytes 2621440 | tf_op jit(solution)/shard_map/reduce_scatter | solution.py:52
  479.8 3.5 copy-start.2
  587.9 20.1 %slice-start = ((s8[6291456]{0:T(1024)(128)(4,1)}), s8[4194304]{0:T(1024)(128)(4,1)S(1)}, s32[]{:S(2)}) async-start(s8[6291456]{0:T(1024)(128)(4,1)} %bitcast.58), calls=%async_computation.10 | async-start | bytes 8388608
  597.0 11.0 %slice-start.1 = ((s8[6291456]{0:T(1024)(128)(4,1)}), s8[2097152]{0:T(1024)(128)(4,1)S(1)}, s32[]{:S(2)}) async-start(s8[6291456]{0:T(1024)(128)(4,1)} %bitcast.58), calls=%async_computation.11 | async-start | bytes 4194304
Sparse Core Ops, SparseCore 0:
  29.7 22.5 all-gather.4
  172.7 16.6 all-gather.2
  466.8 44.4 reduce-scatter.2
  514.5 31.4 reduce-scatter.4
where the time goes:
time: 645 us; the launch traced here: 633 us
  waiting for transfers between devices  422 us (65%)
  local copies, waits for them, and re-layouts  74.7 us (12%)
  matrix products  59.1 us (9%)
  other arithmetic  31.3 us (5%)
  starting transfers between devices  31.2 us (5%)
  between operations  14.3 us (2%)
    all_to_all x1, waiting for transfers between devices, body(): lax.all_to_all(back_cols, 'seq', split_axis=1, concat_axis=2, tiled=True)  107 us
    all_to_all x1, waiting for transfers between devices, body(): lax.all_to_all(product, 'seq', split_axis=1, concat_axis=2, tiled=True)  95.5 us
    all_to_all x1, waiting for transfers between devices, body(): lax.all_to_all(line_combined_result, 'seq', split_axis=2, concat_axis=1,...  92.4 us
    all_to_all x1, waiting for transfers between devices, body(): lax.all_to_all(upstream_rows, 'seq', split_axis=2, concat_axis=1, tiled=T...  92.3 us
    all_gather x1, waiting for transfers between devices, body(): lax.all_gather(first_factor, 'dp', axis=0, tiled=True)  24.6 us
    convert_element_type x1, other arithmetic, body(): grad_input = (block_folded.reshape(sequences, tok_rows, channels) + gate_...  15.1 us
  transfers between devices with their start and end apart: 8, of which 6 were waited for; matrix products, arithmetic and copies ran while one was open for 23% of the time, Pallas kernels for 0%

commit v1 on v0

v1 whole, which is shorter than its diff:
```python
import jax
import jax.numpy as jnp
from jax import lax
from jax.sharding import PartitionSpec as P

LEVELS = 4
PARTS = 3
AXES = ("dp", "seq")


def silu_slope(values):
    logistic = jax.nn.sigmoid(values)
    return logistic * (1.0 + values * (1.0 - logistic))


def body(inputs, cotangent, first_factor, second_factor):
    dp, seq = lax.axis_size("dp"), lax.axis_size("seq")
    ys, xs = dp // 2, seq // LEVELS
    group = 2 * xs
    sequences, tokens, channels = inputs.shape
    assert sequences == 1 and dp % 2 == 0 and seq % LEVELS == 0
    rows1, blocks, size1 = first_factor.shape
    rows2, places, size2 = second_factor.shape
    half = channels // 2
    part = half // PARTS
    mean_weight = 1.0 / (sequences * dp)

    def flat(y, c, z, x):
        return (2 * y + c) * seq + z * xs + x

    def pairs(to):
        return [
            (flat(y, c, z, x), flat(*to(y, c, z, x)))
            for y in range(ys)
            for c in range(2)
            for z in range(LEVELS)
            for x in range(xs)
        ]

    def permute(value, perm):
        return lax.ppermute(value, AXES, perm)

    there = [pairs(lambda y, c, z, x: (y, z % 2, 2 * c + (k ^ (z // 2)), x)) for k in range(2)]
    back = [[(b, a) for a, b in perm] for perm in there]
    swap = pairs(lambda y, c, z, x: (y, z % 2, 2 * (z // 2) + c, x))
    far = pairs(lambda y, c, z, x: (y, c, z ^ 2, x))
    near = pairs(lambda y, c, z, x: (y, c, z ^ 1, x))
    groups = [
        [flat(y, c, z, x) for c in range(2) for x in range(xs)]
        for y in range(ys)
        for z in range(LEVELS)
    ]

    me_y = lax.axis_index("dp") // 2
    me_z = lax.axis_index("seq") // xs
    hi, lo = me_z // 2, me_z % 2

    def ordered(mine, other, bit, axis=0):
        return jnp.where(
            bit == 0, jnp.stack([mine, other], axis), jnp.stack([other, mine], axis)
        )

    def gather(piece, by_slot):
        mine = permute(piece, swap)
        bit = hi ^ lo if by_slot else hi
        mine = ordered(mine, permute(mine, far), bit)
        sent = mine[::-1] if by_slot else mine
        mine = ordered(mine, permute(sent, near), lo)
        step = 1
        while step < ys:
            other = permute(mine, pairs(lambda y, c, z, x: (y ^ step, c, z, x)))
            mine = ordered(mine, other, (me_y // step) % 2)
            step *= 2
        return mine.reshape((dp, 2) + piece.shape)

    def choose(pair, bit):
        return jnp.where(bit == 0, pair[0], pair[1])

    def reduce(whole, by_slot):
        mine = whole.reshape((2,) * (ys.bit_length() - 1) + (2, 2) + whole.shape[2:])
        step = ys // 2
        while step >= 1:
            bit = (me_y // step) % 2
            sent = choose((mine[1], mine[0]), bit).astype(jnp.bfloat16)
            kept = choose((mine[0], mine[1]), bit)
            mine = kept + permute(
                sent, pairs(lambda y, c, z, x: (y ^ step, c, z, x))
            ).astype(jnp.float32)
            step //= 2
        sent = choose((mine[1], mine[0]), lo).astype(jnp.bfloat16)
        sent = sent[::-1] if by_slot else sent
        mine = choose((mine[0], mine[1]), lo) + permute(sent, near).astype(jnp.float32)
        bit = hi ^ lo if by_slot else hi
        sent = choose((mine[1], mine[0]), bit).astype(jnp.bfloat16)
        mine = choose((mine[0], mine[1]), bit) + permute(sent, far).astype(jnp.float32)
        return permute(mine.astype(jnp.bfloat16), swap).astype(jnp.float32)

    def to_columns(value):
        value = value.reshape(2, blocks, 2, group, places, part)
        value = lax.all_to_all(value, AXES, 3, 1, axis_index_groups=groups)
        return value.reshape(size2, 2 * places, part)

    def to_rows(value):
        value = value.reshape(2, group, blocks, 2, places, part)
        value = lax.all_to_all(value, AXES, 1, 3, axis_index_groups=groups)
        return value.reshape(2 * blocks, size1, part)

    def half_swap(value, axes):
        swapped = value
        for axis in axes:
            first, second = jnp.split(swapped, 2, axis)
            swapped = jnp.concatenate([second, first], axis)
        return jnp.where(lo == 0, value, swapped)

    first = gather(first_factor.transpose(1, 0, 2), True)
    first = first.transpose(1, 2, 0, 3, 4).reshape(2 * blocks, size1, size1)
    second = gather(second_factor.transpose(1, 0, 2), False)
    second = second.transpose(1, 2, 0, 3, 4).reshape(2 * places, size2, size2)
    second = half_swap(second, (1, 2))

    def bring(array, q):
        array = array.reshape(blocks, size1, channels)
        slots = []
        for k in range(2):
            start = (k ^ hi) * half + q * part
            piece = lax.dynamic_slice(array, (0, 0, start), (blocks, size1, part))
            slots.append(permute(piece, there[k]))
        return jnp.concatenate(slots, 0)

    x_parts = [bring(inputs, q) for q in range(PARTS)]
    c_parts = [bring(cotangent, q) for q in range(PARTS)]

    first_sum, second_sum, returned = 0.0, 0.0, []
    wide = dict(preferred_element_type=jnp.float32)
    for x_part, c_part in zip(x_parts, c_parts):
        mixed = jnp.einsum("bik,bkd->bid", first, x_part, **wide).astype(jnp.bfloat16)
        columns = to_columns(mixed)
        product = jnp.einsum("jik,kjd->ijd", second, columns, **wide).astype(jnp.bfloat16)
        output = to_rows(product)
        x_wide, c_wide = x_part.astype(jnp.float32), c_part.astype(jnp.float32)
        upstream = (c_wide * jax.nn.silu(x_wide)).astype(jnp.bfloat16)
        up_columns = to_columns(upstream)
        back_columns = jnp.einsum("jik,ijd->kjd", second, up_columns, **wide).astype(jnp.bfloat16)
        mixed_grad = to_rows(back_columns)
        second_sum += jnp.einsum("ijd,kjd->jik", up_columns, columns, **wide)
        first_sum += jnp.einsum("bid,bkd->bik", mixed_grad, x_part, **wide)
        gate_term = (c_wide * output.astype(jnp.float32) * silu_slope(x_wide)).astype(jnp.bfloat16)
        folded = jnp.einsum("bik,bid->bkd", first, mixed_grad, **wide)
        grad = (folded + gate_term.astype(jnp.float32)).astype(jnp.bfloat16)
        grad = grad.reshape(2, blocks, size1, part)
        returned.append([permute(grad[k], back[k]) for k in range(2)])

    first_sum = (first_sum * mean_weight).reshape(2, blocks, dp, rows1, size1)
    first_grad = reduce(first_sum.transpose(2, 0, 1, 3, 4), True).transpose(1, 0, 2)
    second_sum = half_swap(second_sum * mean_weight, (1, 2)).reshape(2, places, dp, rows2, size2)
    second_grad = reduce(second_sum.transpose(2, 0, 1, 3, 4), False).transpose(1, 0, 2)
    slots = [jnp.concatenate([r[k] for r in returned], -1) for k in range(2)]
    grad_input = jnp.where(
        hi == 0, jnp.concatenate(slots, -1), jnp.concatenate(slots[::-1], -1)
    ).reshape(1, tokens, channels)
    return (grad_input, first_grad, second_grad)


def solution(mesh):
    placed = P("dp", "seq", None)
    return jax.shard_map(
        body,
        mesh=mesh,
        in_specs=(placed,) * 4,
        out_specs=(placed,) * 3,
        check_vma=False,
    )
```

time: 645 us -> 826 us (1.28)
  starting transfers between devices: 31.2 us -> 224 us
  waiting for transfers between devices: 422 us -> 334 us
  other arithmetic: 31.3 us -> 89.9 us
  local copies, waits for them, and re-layouts: 74.7 us -> 99.8 us
  between operations: 14.3 us -> 2.46 us
    all_to_all x4 -> x12, waiting for transfers between devices: 387 us -> 80.8 us  [the longest x6 43.7 us: to_rows(): value = lax.all_to_all(value, AXES, 1, 3, axis_index_groups=groups)]
    ppermute x0 -> x34, waiting for transfers between devices: none -> 253 us  [permute(): return lax.ppermute(value, AXES, perm)]
    ppermute x0 -> x34, starting transfers between devices: none -> 169 us  [permute(): return lax.ppermute(value, AXES, perm)]
    all_gather x2 -> x0, waiting for transfers between devices: 35.1 us -> none  [the longest x1 24.6 us: body(): lax.all_gather(first_factor, 'dp', axis=0, tiled=True)]
    convert_element_type x3 -> x0, local copies, waits for them, and re-layouts: 27.1 us -> none  [the longest x1 9.08 us: body(): product = jnp.einsum('ijk,skjd->sijd', second_full, columns, preferred_el...]
    select_n x0 -> x13, other arithmetic: none -> 26.8 us  [the longest x10 15.8 us: ordered(): jnp.where(bit == 0, jnp.stack([mine, other], axis), jnp.stack([other, min...]
    all_to_all x4 -> x12, starting transfers between devices: 30.8 us -> 54.5 us  [the longest x6 27.6 us: to_rows(): value = lax.all_to_all(value, AXES, 1, 3, axis_index_groups=groups)]
    another operation x0 -> x9, local copies, waits for them, and re-layouts: none -> 19.2 us  [the longest x6 13.4 us: to_rows(): value = lax.all_to_all(value, AXES, 1, 3, axis_index_groups=groups)]
  transfers between devices with their start and end apart: 8 -> 46, of which waited for: 6 -> 19; matrix products, arithmetic and copies ran while one was open for 23% -> 28% of each run, Pallas kernels for 0% -> 0%
where the time goes in v1:
time: 826 us; the launch traced here: 812 us
  waiting for transfers between devices  334 us (40%)
  starting transfers between devices  224 us (27%)
  local copies, waits for them, and re-layouts  99.8 us (12%)
  other arithmetic  89.9 us (11%)
  matrix products  62.9 us (8%)
    ppermute x34, waiting for transfers between devices, permute(): return lax.ppermute(value, AXES, perm)  253 us
    ppermute x34, starting transfers between devices, permute(): return lax.ppermute(value, AXES, perm)  169 us
    all_to_all x6, waiting for transfers between devices, to_rows(): value = lax.all_to_all(value, AXES, 1, 3, axis_index_groups=groups)  43.7 us
    all_to_all x6, waiting for transfers between devices, to_columns(): value = lax.all_to_all(value, AXES, 3, 1, axis_index_groups=groups)  37.1 us
    all_to_all x6, starting transfers between devices, to_rows(): value = lax.all_to_all(value, AXES, 1, 3, axis_index_groups=groups)  27.6 us
    all_to_all x6, starting transfers between devices, to_columns(): value = lax.all_to_all(value, AXES, 3, 1, axis_index_groups=groups)  26.9 us
    convert_element_type x3, other arithmetic, body(): upstream = (c_wide * jax.nn.silu(x_wide)).astype(jnp.bfloat16)  23.7 us
    unnamed x90, local copies, waits for them, and re-layouts  18.4 us
  transfers between devices with their start and end apart: 46, of which 19 were waited for; matrix products, arithmetic and copies ran while one was open for 28% of the time, Pallas kernels for 0%

profile of v1, /device:TPU:20, one launch (start us, length us, event | category | flops | bytes accessed | tf_op | source)
XLA Modules:
  0.0 812.1 jit_solution(9535996636087530016)
XLA Ops:
  0.7 5.7 constant_dynamic-slice_fusion
  15.0 7.9 collective-permute-start.14
  24.9 9.8 %collective-permute-done.15 = bf16[16,256,128]{2,1,0:T(8,128)(2,1)S(1)} collective-permute-done((bf16[16,256,128]{2,1,0:T(8,128)(2,1)S(1)}, bf16[16,256,128]{2,1,0:T(8,128)(2,1)S(1)}, u32[]{:S(2)}, u32[]{:S(2)}) %collective-permute-start.15) | collective-permute-done | bytes 1048608 | tf_op jit(solution)/shard_map/ppermute | solution.py:41
  35.4 20.3 %collective-permute-done.16 = bf16[16,256,128]{2,1,0:T(8,128)(2,1)S(1)} collective-permute-done((bf16[16,256,128]{2,1,0:T(8,128)(2,1)}, bf16[16,256,128]{2,1,0:T(8,128)(2,1)S(1)}, u32[]{:S(2)}, u32[]{:S(2)}) %collective-permute-start.16) | collective-permute-done | bytes 1048608 | tf_op jit(solution)/shard_map/ppermute | solution.py:41
  60.5 46.6 %collective-permute-start.4 = (bf16[16,256,128]{2,1,0:T(8,128)(2,1)}, bf16[16,256,128]{2,1,0:T(8,128)(2,1)}, u32[]{:S(2)}, u32[]{:S(2)}) collective-permute-start(bf16[16,256,128]{2,1,0:T(8,128)(2,1)} %get-tuple-element.14), channel_id=1, source_target_pairs={{0,0},{1,1},{2,8},{3,9},{4,2},{5,3},{6,10},{7,11},{8,4},{9,5},{10,... | collective-permute-start | bytes 3145736 | tf_op jit(solution)/shard_map/ppermute | solution.py:41
  107.3 21.8 %collective-permute-done.14 = bf16[16,256,128]{2,1,0:T(8,128)(2,1)} collective-permute-done((bf16[16,256,128]{2,1,0:T(8,128)(2,1)}, bf16[16,256,128]{2,1,0:T(8,128)(2,1)}, u32[]{:S(2)}, u32[]{:S(2)}) %collective-permute-start.14) | collective-permute-done | bytes 1048608 | tf_op jit(solution)/shard_map/ppermute | solution.py:41
  134.4 7.9 fusion.3
  145.9 55.0 %collective-permute-done.9 = bf16[32,32,128]{2,0,1:T(8,128)(2,1)S(1)} collective-permute-done((bf16[32,32,128]{2,0,1:T(8,128)(2,1)S(1)}, bf16[32,32,128]{2,0,1:T(8,128)(2,1)S(1)}, u32[]{:S(2)}, u32[]{:S(2)}) %collective-permute-start.9) | collective-permute-done | bytes 262176 | tf_op jit(solution)/shard_map/ppermute | solution.py:41
  207.6 11.0 %collective-permute-start.21 = (bf16[16,256,128]{2,1,0:T(8,128)(2,1)}, bf16[16,256,128]{2,1,0:T(8,128)(2,1)}, u32[]{:S(2)}, u32[]{:S(2)}) collective-permute-start(bf16[16,256,128]{2,1,0:T(8,128)(2,1)} %get-tuple-element.3), channel_id=1, source_target_pairs={{0,2},{1,3},{2,10},{3,11},{4,0},{5,1},{6,8},{7,9},{8,6},{9,7},{10,... | collective-permute-start | bytes 3145736 | tf_op jit(solution)/shard_map/ppermute | solution.py:41
  223.4 7.6 collective-permute-start.19
  232.9 7.9 fusion.4
  247.1 41.3 %collective-permute-done.10 = bf16[2,32,32,128]{3,1,2,0:T(8,128)(2,1)} collective-permute-done((bf16[2,32,32,128]{3,1,2,0:T(8,128)(2,1)}, bf16[2,32,32,128]{3,1,2,0:T(8,128)(2,1)}, u32[]{:S(2)}, u32[]{:S(2)}) %collective-permute-start.10) | collective-permute-done | bytes 524320 | tf_op jit(solution)/shard_map/ppermute | solution.py:41
  292.6 21.8 %collective-permute-done.19 = bf16[16,256,128]{2,1,0:T(8,128)(2,1)} collective-permute-done((bf16[16,256,128]{2,1,0:T(8,128)(2,1)}, bf16[16,256,128]{2,1,0:T(8,128)(2,1)}, u32[]{:S(2)}, u32[]{:S(2)}) %collective-permute-start.19) | collective-permute-done | bytes 1048608 | tf_op jit(solution)/shard_map/ppermute | solution.py:41
  319.0 7.9 fusion.2
  340.4 17.0 %all-to-all-done.8 = bf16[2,1,16,2,4,32,128]{6,2,0,5,3,1,4:T(8,128)(2,1)} async-done(((bf16[2,1,16,2,4,32,128]{6,2,0,5,3,1,4:T(8,128)(2,1)}), bf16[2,1,16,2,4,32,128]{6,2,0,5,3,1,4:T(8,128)(2,1)}, u32[]{:S(2)}, u32[]{:S(2)}) %all-to-all-start.8) | async-done | bytes 2097184 | tf_op jit(solution)/shard_map/all_to_all | solution.py:100
  371.7 15.9 %all-to-all-done.5 = bf16[2,4,16,2,1,32,128]{6,2,0,5,3,4,1:T(8,128)(2,1)} async-done(((bf16[2,4,16,2,1,32,128]{6,2,0,5,3,4,1:T(8,128)(2,1)}), bf16[2,4,16,2,1,32,128]{6,2,0,5,3,4,1:T(8,128)(2,1)}, u32[]{:S(2)}, u32[]{:S(2)}) %all-to-all-start.5) | async-done | bytes 2097184 | tf_op jit(solution)/shard_map/all_to_all | solution.py:105
  402.0 15.9 %all-to-all-done.1 = bf16[2,4,16,2,1,32,128]{6,2,0,5,3,4,1:T(8,128)(2,1)} async-done(((bf16[2,4,16,2,1,32,128]{6,2,0,5,3,4,1:T(8,128)(2,1)}), bf16[2,4,16,2,1,32,128]{6,2,0,5,3,4,1:T(8,128)(2,1)}, u32[]{:S(2)}, u32[]{:S(2)}) %all-to-all-start.1) | async-done | bytes 2097184 | tf_op jit(solution)/shard_map/all_to_all | solution.py:105
  424.6 19.8 %collective-permute-done.3 = bf16[2,2,16,64,256]{4,2,3,1,0:T(8,128)(2,1)} collective-permute-done((bf16[2,2,16,64,256]{4,2,3,1,0:T(8,128)(2,1)}, bf16[2,2,16,64,256]{4,2,3,1,0:T(8,128)(2,1)}, u32[]{:S(2)}, u32[]{:S(2)}) %collective-permute-start.3) | collective-permute-done | bytes 2097184 | tf_op jit(solution)/shard_map/ppermute | solution.py:41
  463.2 19.7 %all-to-all-done.6 = bf16[2,1,16,2,4,32,128]{6,5,3,2,0,1,4:T(8,128)(2,1)} async-done(((bf16[2,1,16,2,4,32,128]{6,5,3,2,0,1,4:T(8,128)(2,1)}), bf16[2,1,16,2,4,32,128]{6,5,3,2,0,1,4:T(8,128)(2,1)}, u32[]{:S(2)}, u32[]{:S(2)}) %all-to-all-start.6) | async-done | bytes 2097184 | tf_op jit(solution)/shard_map/all_to_all | solution.py:100
  517.9 8.3 %add_multiply_fusion = f32[32,256,256]{2,1,0:T(8,128)S(1)} fusion(f32[32,256,256]{2,1,0:T(8,128)} %fusion.18, f32[32,256,256]{2,1,0:T(8,128)} %fusion.19, bf16[32,256,128]{2,1,0:T(8,128)(2,1)} %bitcast.242, bf16[32,256,128]{2,1,0:T(8,128)(2,1)} %copy-done.6), kind=kOutput, calls=%fused_computation.1 | convolution fusion | flops 543162368 | bytes 29360128 | tf_op jit(solution)/shard_map/bid,bkd->bik/dot_general | solution.py:146
  576.3 5.4 collective-permute-done.26
  581.8 5.3 convert_add_fusion
  610.3 5.8 collective-permute-done.27
  623.3 7.7 collective-permute-done.31
  644.7 7.4 add_convert_fusion
  658.5 11.9 %all-to-all-done.3 = bf16[2,4,16,2,1,32,128]{6,5,3,2,0,4,1:T(8,128)(2,1)} async-done(((bf16[2,4,16,2,1,32,128]{6,5,3,2,0,4,1:T(8,128)(2,1)}), bf16[2,4,16,2,1,32,128]{6,5,3,2,0,4,1:T(8,128)(2,1)}, u32[]{:S(2)}, u32[]{:S(2)}) %all-to-all-start.3) | async-done | bytes 2097184 | tf_op jit(solution)/shard_map/all_to_all | solution.py:105
  676.1 5.5 add_convert_fusion.2
  696.8 51.0 %collective-permute-start.17 = (bf16[16,256,128]{2,1,0:T(8,128)(2,1)S(1)}, bf16[16,256,128]{2,1,0:T(8,128)(2,1)S(1)}, u32[]{:S(2)}, u32[]{:S(2)}) collective-permute-start(bf16[16,256,128]{2,1,0:T(8,128)(2,1)S(1)} %get-tuple-element.20), channel_id=1, source_target_pairs={{0,0},{1,1},{8,2},{9,3},{2,4},{3,5},{10,6},{11,7},{4,8},{5,9},{12,... | collective-permute-start | bytes 3145736 | tf_op jit(solution)/shard_map/ppermute | solution.py:41
  753.2 5.6 collective-permute-start.29
  760.5 16.9 %collective-permute-done.17 = bf16[16,256,128]{2,1,0:T(8,128)(2,1)S(1)} collective-permute-done((bf16[16,256,128]{2,1,0:T(8,128)(2,1)S(1)}, bf16[16,256,128]{2,1,0:T(8,128)(2,1)S(1)}, u32[]{:S(2)}, u32[]{:S(2)}) %collective-permute-start.17) | collective-permute-done | bytes 1048608 | tf_op jit(solution)/shard_map/ppermute | solution.py:41
  777.9 22.0 %collective-permute-done.22 = bf16[16,256,128]{2,1,0:T(8,128)(2,1)S(1)} collective-permute-done((bf16[16,256,128]{2,1,0:T(8,128)(2,1)}, bf16[16,256,128]{2,1,0:T(8,128)(2,1)S(1)}, u32[]{:S(2)}, u32[]{:S(2)}) %collective-permute-start.22) | collective-permute-done | bytes 1048608 | tf_op jit(solution)/shard_map/ppermute | solution.py:41
  803.1 6.3 broadcast_select_fusion
  (251 shorter events, 289.8 us)
Async XLA Ops:
  8.7 46.9 %collective-permute-start.16 = (bf16[16,256,128]{2,1,0:T(8,128)(2,1)}, bf16[16,256,128]{2,1,0:T(8,128)(2,1)S(1)}, u32[]{:S(2)}, u32[]{:S(2)}) collective-permute-start(bf16[16,256,128]{2,1,0:T(8,128)(2,1)} %get-tuple-element.5), channel_id=1, source_target_pairs={{0,2},{1,3},{2,10},{3,11},{4,0},{5,1},{6,8},{7,9},{8,6},{9,7},{10,... | collective-permute-start | bytes 3145736 | tf_op jit(solution)/shard_map/ppermute | solution.py:41
  12.0 95.2 %collective-permute-start.13 = (bf16[16,256,128]{2,1,0:T(8,128)(2,1)}, bf16[16,256,128]{2,1,0:T(8,128)(2,1)}, u32[]{:S(2)}, u32[]{:S(2)}) collective-permute-start(bf16[16,256,128]{2,1,0:T(8,128)(2,1)} %get-tuple-element.12), channel_id=1, source_target_pairs={{0,0},{1,1},{2,8},{3,9},{4,2},{5,3},{6,10},{7,11},{8,4},{9,5},{10,... | collective-permute-start | bytes 3145736 | tf_op jit(solution)/shard_map/ppermute | solution.py:41
  15.0 114.1 %collective-permute-start.14 = (bf16[16,256,128]{2,1,0:T(8,128)(2,1)}, bf16[16,256,128]{2,1,0:T(8,128)(2,1)}, u32[]{:S(2)}, u32[]{:S(2)}) collective-permute-start(bf16[16,256,128]{2,1,0:T(8,128)(2,1)} %get-tuple-element.11), channel_id=1, source_target_pairs={{0,2},{1,3},{2,10},{3,11},{4,0},{5,1},{6,8},{7,9},{8,6},{9,7},{10,... | collective-permute-start | bytes 3145736 | tf_op jit(solution)/shard_map/ppermute | solution.py:41
  22.9 181.5 %collective-permute-start.6 = (bf16[16,256,128]{2,1,0:T(8,128)(2,1)}, bf16[16,256,128]{2,1,0:T(8,128)(2,1)}, u32[]{:S(2)}, u32[]{:S(2)}) collective-permute-start(bf16[16,256,128]{2,1,0:T(8,128)(2,1)} %get-tuple-element.8), channel_id=1, source_target_pairs={{0,0},{1,1},{2,8},{3,9},{4,2},{5,3},{6,10},{7,11},{8,4},{9,5},{10,... | collective-permute-start | bytes 3145736 | tf_op jit(solution)/shard_map/ppermute | solution.py:41
  55.6 151.9 %collective-permute-start.7 = (bf16[16,256,128]{2,1,0:T(8,128)(2,1)}, bf16[16,256,128]{2,1,0:T(8,128)(2,1)}, u32[]{:S(2)}, u32[]{:S(2)}) collective-permute-start(bf16[16,256,128]{2,1,0:T(8,128)(2,1)} %get-tuple-element.7), channel_id=1, source_target_pairs={{0,2},{1,3},{2,10},{3,11},{4,0},{5,1},{6,8},{7,9},{8,6},{9,7},{10,... | collective-permute-start | bytes 3145736 | tf_op jit(solution)/shard_map/ppermute | solution.py:41
  60.5 160.8 %collective-permute-start.4 = (bf16[16,256,128]{2,1,0:T(8,128)(2,1)}, bf16[16,256,128]{2,1,0:T(8,128)(2,1)}, u32[]{:S(2)}, u32[]{:S(2)}) collective-permute-start(bf16[16,256,128]{2,1,0:T(8,128)(2,1)} %get-tuple-element.14), channel_id=1, source_target_pairs={{0,0},{1,1},{2,8},{3,9},{4,2},{5,3},{6,10},{7,11},{8,4},{9,5},{10,... | collective-permute-start | bytes 3145736 | tf_op jit(solution)/shard_map/ppermute | solution.py:41
  107.2 116.2 %collective-permute-start.5 = (bf16[16,256,128]{2,1,0:T(8,128)(2,1)}, bf16[16,256,128]{2,1,0:T(8,128)(2,1)}, u32[]{:S(2)}, u32[]{:S(2)}) collective-permute-start(bf16[16,256,128]{2,1,0:T(8,128)(2,1)} %get-tuple-element.13), channel_id=1, source_target_pairs={{0,2},{1,3},{2,10},{3,11},{4,0},{5,1},{6,8},{7,9},{8,6},{9,7},{10,... | collective-permute-start | bytes 3145736 | tf_op jit(solution)/shard_map/ppermute | solution.py:41
  129.1 71.9 %collective-permute-start.9 = (bf16[32,32,128]{2,0,1:T(8,128)(2,1)S(1)}, bf16[32,32,128]{2,0,1:T(8,128)(2,1)S(1)}, u32[]{:S(2)}, u32[]{:S(2)}) collective-permute-start(bf16[32,32,128]{2,0,1:T(8,128)(2,1)S(1)} %collective-permute-done.8), channel_id=1, source_target_pairs={{0,4},{1,5},{2,6},{3,7},{4,0},{5,1},{6,2},{7,3},{8,12},{9,13},{10,... | collective-permute-start | bytes 786440 | tf_op jit(solution)/shard_map/ppermute | solution.py:41
  142.3 98.5 %all-to-all-start.4 = ((bf16[2,1,16,2,4,32,128]{6,2,0,5,3,1,4:T(8,128)(2,1)}), bf16[2,1,16,2,4,32,128]{6,2,0,5,3,1,4:T(8,128)(2,1)S(1)}, u32[]{:S(2)}, u32[]{:S(2)}) async-start(bf16[2,1,16,2,4,32,128]{6,2,0,5,3,1,4:T(8,128)(2,1)} %fusion.3), calls=%async_computation.4 | async-start | bytes 4194304 | tf_op jit(solution)/shard_map/all_to_all | solution.py:100
  204.4 86.4 %collective-permute-start.20 = (bf16[16,256,128]{2,1,0:T(8,128)(2,1)}, bf16[16,256,128]{2,1,0:T(8,128)(2,1)}, u32[]{:S(2)}, u32[]{:S(2)}) collective-permute-start(bf16[16,256,128]{2,1,0:T(8,128)(2,1)} %get-tuple-element.4), channel_id=1, source_target_pairs={{0,0},{1,1},{2,8},{3,9},{4,2},{5,3},{6,10},{7,11},{8,4},{9,5},{10,... | collective-permute-start | bytes 3145736 | tf_op jit(solution)/shard_map/ppermute | solution.py:41
  207.6 108.7 %collective-permute-start.21 = (bf16[16,256,128]{2,1,0:T(8,128)(2,1)}, bf16[16,256,128]{2,1,0:T(8,128)(2,1)}, u32[]{:S(2)}, u32[]{:S(2)}) collective-permute-start(bf16[16,256,128]{2,1,0:T(8,128)(2,1)} %get-tuple-element.3), channel_id=1, source_target_pairs={{0,2},{1,3},{2,10},{3,11},{4,0},{5,1},{6,8},{7,9},{8,6},{9,7},{10,... | collective-permute-start | bytes 3145736 | tf_op jit(solution)/shard_map/ppermute | solution.py:41
  221.3 71.3 %collective-permute-start.18 = (bf16[16,256,128]{2,1,0:T(8,128)(2,1)}, bf16[16,256,128]{2,1,0:T(8,128)(2,1)}, u32[]{:S(2)}, u32[]{:S(2)}) collective-permute-start(bf16[16,256,128]{2,1,0:T(8,128)(2,1)} %get-tuple-element.9), channel_id=1, source_target_pairs={{0,0},{1,1},{2,8},{3,9},{4,2},{5,3},{6,10},{7,11},{8,4},{9,5},{10,... | collective-permute-start | bytes 3145736 | tf_op jit(solution)/shard_map/ppermute | solution.py:41
  223.4 91.0 %collective-permute-start.19 = (bf16[16,256,128]{2,1,0:T(8,128)(2,1)}, bf16[16,256,128]{2,1,0:T(8,128)(2,1)}, u32[]{:S(2)}, u32[]{:S(2)}) collective-permute-start(bf16[16,256,128]{2,1,0:T(8,128)(2,1)} %get-tuple-element.10), channel_id=1, source_target_pairs={{0,2},{1,3},{2,10},{3,11},{4,0},{5,1},{6,8},{7,9},{8,6},{9,7},{10,... | collective-permute-start | bytes 3145736 | tf_op jit(solution)/shard_map/ppermute | solution.py:41
  232.8 55.6 %collective-permute-start.10 = (bf16[2,32,32,128]{3,1,2,0:T(8,128)(2,1)}, bf16[2,32,32,128]{3,1,2,0:T(8,128)(2,1)}, u32[]{:S(2)}, u32[]{:S(2)}) collective-permute-start(bf16[2,32,32,128]{3,1,2,0:T(8,128)(2,1)} %maximum_select_fusion.9), channel_id=1, source_target_pairs={{0,2},{1,3},{2,0},{3,1},{4,6},{5,7},{6,4},{7,5},{8,10},{9,11},{10,... | collective-permute-start | bytes 1572872 | tf_op jit(solution)/shard_map/ppermute | solution.py:41
  242.2 84.7 %all-to-all-start = ((bf16[2,1,16,2,4,32,128]{6,2,0,5,3,1,4:T(8,128)(2,1)}), bf16[2,1,16,2,4,32,128]{6,2,0,5,3,1,4:T(8,128)(2,1)}, u32[]{:S(2)}, u32[]{:S(2)}) async-start(bf16[2,1,16,2,4,32,128]{6,2,0,5,3,1,4:T(8,128)(2,1)} %fusion.4), calls=%async_computation | async-start | bytes 4194304 | tf_op jit(solution)/shard_map/all_to_all | solution.py:100
  288.4 73.5 %collective-permute-start.1 = (bf16[16,64,256]{2,0,1:T(8,128)(2,1)S(1)}, bf16[16,64,256]{2,0,1:T(8,128)(2,1)S(1)}, u32[]{:S(2)}, u32[]{:S(2)}) collective-permute-start(bf16[16,64,256]{2,0,1:T(8,128)(2,1)S(1)} %collective-permute-done), channel_id=1, source_target_pairs={{0,4},{1,5},{2,6},{3,7},{4,0},{5,1},{6,2},{7,3},{8,12},{9,13},{10,... | collective-permute-start | bytes 1572872 | tf_op jit(solution)/shard_map/ppermute | solution.py:41
  290.8 42.3 %collective-permute-start.11 = (bf16[2,2,32,32,128]{4,2,3,1,0:T(8,128)(2,1)}, bf16[2,2,32,32,128]{4,2,3,1,0:T(8,128)(2,1)S(1)}, u32[]{:S(2)}, u32[]{:S(2)}) collective-permute-start(bf16[2,2,32,32,128]{4,2,3,1,0:T(8,128)(2,1)} %maximum_select_fusion.7), channel_id=1, source_target_pairs={{0,16},{1,17},{2,18},{3,19},{4,20},{5,21},{6,22},{7,23},{8,24},{9,... | collective-permute-start | bytes 3145736 | tf_op jit(solution)/shard_map/ppermute | solution.py:41
  396.1 48.3 %collective-permute-start.3 = (bf16[2,2,16,64,256]{4,2,3,1,0:T(8,128)(2,1)}, bf16[2,2,16,64,256]{4,2,3,1,0:T(8,128)(2,1)}, u32[]{:S(2)}, u32[]{:S(2)}) collective-permute-start(bf16[2,2,16,64,256]{4,2,3,1,0:T(8,128)(2,1)} %maximum_select_fusion.2), channel_id=1, source_target_pairs={{0,16},{1,17},{2,18},{3,19},{4,20},{5,21},{6,22},{7,23},{8,24},{9,... | collective-permute-start | bytes 6291464 | tf_op jit(solution)/shard_map/ppermute | solution.py:41
  417.9 34.8 %all-to-all-start.9 = ((bf16[2,4,16,2,1,32,128]{6,2,0,5,3,4,1:T(8,128)(2,1)}), bf16[2,4,16,2,1,32,128]{6,2,0,5,3,4,1:T(8,128)(2,1)}, u32[]{:S(2)}, u32[]{:S(2)}) async-start(bf16[2,4,16,2,1,32,128]{6,2,0,5,3,4,1:T(8,128)(2,1)} %copy.66), calls=%async_computation.9 | async-start | bytes 4194304 | tf_op jit(solution)/shard_map/all_to_all | solution.py:105
  513.1 35.4 %all-to-all-start.10 = ((bf16[2,1,16,2,4,32,128]{6,5,3,2,0,1,4:T(8,128)(2,1)}), bf16[2,1,16,2,4,32,128]{6,5,3,2,0,1,4:T(8,128)(2,1)}, u32[]{:S(2)}, u32[]{:S(2)}) async-start(bf16[2,1,16,2,4,32,128]{6,5,3,2,0,1,4:T(8,128)(2,1)} %copy.69), calls=%async_computation.10 | async-start | bytes 4194304 | tf_op jit(solution)/shard_map/all_to_all | solution.py:100
  533.0 48.7 %collective-permute-start.26 = (bf16[2,2,16,64,256]{4,2,3,1,0:T(8,128)(2,1)}, bf16[2,2,16,64,256]{4,2,3,1,0:T(8,128)(2,1)}, u32[]{:S(2)}, u32[]{:S(2)}) collective-permute-start(bf16[2,2,16,64,256]{4,2,3,1,0:T(8,128)(2,1)} %select_convert_fusion), channel_id=1, source_target_pairs={{0,16},{1,17},{2,18},{3,19},{4,20},{5,21},{6,22},{7,23},{8,24},{9,... | collective-permute-start | bytes 6291464 | tf_op jit(solution)/shard_map/ppermute | solution.py:41
  567.8 36.0 %collective-permute-start.30 = (bf16[2,2,32,32,128]{4,2,3,1,0:T(8,128)(2,1)}, bf16[2,2,32,32,128]{4,2,3,1,0:T(8,128)(2,1)}, u32[]{:S(2)}, u32[]{:S(2)}) collective-permute-start(bf16[2,2,32,32,128]{4,2,3,1,0:T(8,128)(2,1)} %select_convert_fusion.1), channel_id=1, source_target_pairs={{0,16},{1,17},{2,18},{3,19},{4,20},{5,21},{6,22},{7,23},{8,24},{9,... | collective-permute-start | bytes 3145736 | tf_op jit(solution)/shard_map/ppermute | solution.py:41
  605.7 34.2 %all-to-all-start.7 = ((bf16[2,4,16,2,1,32,128]{6,5,3,2,0,4,1:T(8,128)(2,1)}), bf16[2,4,16,2,1,32,128]{6,5,3,2,0,4,1:T(8,128)(2,1)}, u32[]{:S(2)}, u32[]{:S(2)}) async-start(bf16[2,4,16,2,1,32,128]{6,5,3,2,0,4,1:T(8,128)(2,1)} %copy.59), calls=%async_computation.7 | async-start | bytes 4194304 | tf_op jit(solution)/shard_map/all_to_all | solution.py:105
  619.9 74.0 %collective-permute-start.28 = (bf16[16,64,256]{2,0,1:T(8,128)(2,1)}, bf16[16,64,256]{2,0,1:T(8,128)(2,1)}, u32[]{:S(2)}, u32[]{:S(2)}) collective-permute-start(bf16[16,64,256]{2,0,1:T(8,128)(2,1)} %fusion.9), channel_id=1, source_target_pairs={{0,4},{1,5},{2,6},{3,7},{4,0},{5,1},{6,2},{7,3},{8,12},{9,13},{10,... | collective-permute-start | bytes 1572872 | tf_op jit(solution)/shard_map/ppermute | solution.py:41
  632.1 57.0 %collective-permute-start.32 = (bf16[32,32,128]{2,0,1:T(8,128)(2,1)}, bf16[32,32,128]{2,0,1:T(8,128)(2,1)S(1)}, u32[]{:S(2)}, u32[]{:S(2)}) collective-permute-start(bf16[32,32,128]{2,0,1:T(8,128)(2,1)} %fusion.12), channel_id=1, source_target_pairs={{0,4},{1,5},{2,6},{3,7},{4,0},{5,1},{6,2},{7,3},{8,12},{9,13},{10,... | collective-permute-start | bytes 786440 | tf_op jit(solution)/shard_map/ppermute | solution.py:41
  653.2 106.0 %collective-permute-start.25 = (bf16[16,256,128]{2,1,0:T(8,128)(2,1)S(1)}, bf16[16,256,128]{2,1,0:T(8,128)(2,1)S(1)}, u32[]{:S(2)}, u32[]{:S(2)}) collective-permute-start(bf16[16,256,128]{2,1,0:T(8,128)(2,1)S(1)} %get-tuple-element.17), channel_id=1, source_target_pairs={{2,0},{3,1},{10,2},{11,3},{0,4},{1,5},{8,6},{9,7},{6,8},{7,9},{14,... | collective-permute-start | bytes 3145736 | tf_op jit(solution)/shard_map/ppermute | solution.py:41
  684.4 64.3 %collective-permute-start.23 = (bf16[16,256,128]{2,1,0:T(8,128)(2,1)}, bf16[16,256,128]{2,1,0:T(8,128)(2,1)S(1)}, u32[]{:S(2)}, u32[]{:S(2)}) collective-permute-start(bf16[16,256,128]{2,1,0:T(8,128)(2,1)} %get-tuple-element.21), channel_id=1, source_target_pairs={{2,0},{3,1},{10,2},{11,3},{0,4},{1,5},{8,6},{9,7},{6,8},{7,9},{14,... | collective-permute-start | bytes 3145736 | tf_op jit(solution)/shard_map/ppermute | solution.py:41
  689.0 64.2 %collective-permute-start.24 = (bf16[16,256,128]{2,1,0:T(8,128)(2,1)S(1)}, bf16[16,256,128]{2,1,0:T(8,128)(2,1)S(1)}, u32[]{:S(2)}, u32[]{:S(2)}) collective-permute-start(bf16[16,256,128]{2,1,0:T(8,128)(2,1)S(1)} %get-tuple-element.19), channel_id=1, source_target_pairs={{2,0},{3,1},{10,2},{11,3},{0,4},{1,5},{8,6},{9,7},{6,8},{7,9},{14,... | collective-permute-start | bytes 3145736 | tf_op jit(solution)/shard_map/ppermute | solution.py:41
  689.1 70.3 %collective-permute-start.12 = (bf16[16,256,128]{2,1,0:T(8,128)(2,1)S(1)}, bf16[16,256,128]{2,1,0:T(8,128)(2,1)S(1)}, u32[]{:S(2)}, u32[]{:S(2)}) collective-permute-start(bf16[16,256,128]{2,1,0:T(8,128)(2,1)S(1)} %get-tuple-element.22), channel_id=1, source_target_pairs={{0,0},{1,1},{8,2},{9,3},{2,4},{3,5},{10,6},{11,7},{4,8},{5,9},{12,... | collective-permute-start | bytes 3145736 | tf_op jit(solution)/shard_map/ppermute | solution.py:41
  696.8 80.6 %collective-permute-start.17 = (bf16[16,256,128]{2,1,0:T(8,128)(2,1)S(1)}, bf16[16,256,128]{2,1,0:T(8,128)(2,1)S(1)}, u32[]{:S(2)}, u32[]{:S(2)}) collective-permute-start(bf16[16,256,128]{2,1,0:T(8,128)(2,1)S(1)} %get-tuple-element.20), channel_id=1, source_target_pairs={{0,0},{1,1},{8,2},{9,3},{2,4},{3,5},{10,6},{11,7},{4,8},{5,9},{12,... | collective-permute-start | bytes 3145736 | tf_op jit(solution)/shard_map/ppermute | solution.py:41
  748.7 51.2 %collective-permute-start.22 = (bf16[16,256,128]{2,1,0:T(8,128)(2,1)}, bf16[16,256,128]{2,1,0:T(8,128)(2,1)S(1)}, u32[]{:S(2)}, u32[]{:S(2)}) collective-permute-start(bf16[16,256,128]{2,1,0:T(8,128)(2,1)} %get-tuple-element.18), channel_id=1, source_target_pairs={{0,0},{1,1},{8,2},{9,3},{2,4},{3,5},{10,6},{11,7},{4,8},{5,9},{12,... | collective-permute-start | bytes 3145736 | tf_op jit(solution)/shard_map/ppermute | solution.py:41
  753.2 56.2 %collective-permute-start.29 = (bf16[16,64,256]{2,0,1:T(8,128)(2,1)}, bf16[16,64,256]{2,0,1:T(8,128)(2,1)}, u32[]{:S(2)}, u32[]{:S(2)}) collective-permute-start(bf16[16,64,256]{2,0,1:T(8,128)(2,1)} %fusion.8), channel_id=1, source_target_pairs={{0,0},{1,1},{2,8},{3,9},{4,4},{5,5},{6,12},{7,13},{8,2},{9,3},{10,... | collective-permute-start | bytes 1572872 | tf_op jit(solution)/shard_map/ppermute | solution.py:41
  (54 other events, 560.3 us)

commit v2 on v0

v2 whole, which is shorter than its diff:
```python
import jax
import jax.numpy as jnp
from jax import lax
from jax.experimental import pallas as pl
from jax.experimental.pallas import tpu as pltpu
from jax.sharding import PartitionSpec as P

MANY = 2
ROOM = pltpu.CompilerParams(vmem_limit_bytes=56 * 1024 * 1024)


def upstream_kernel(x_ref, c_ref, out_ref):
    owners, many, places, channels = out_ref.shape
    for n in range(many):
        x, c = x_ref[n].astype(jnp.float32), c_ref[n].astype(jnp.float32)
        half = 0.5 * x
        up = c * (half + half * jnp.tanh(half))
        out_ref[:, n] = up.reshape(owners, places, channels).astype(out_ref.dtype)


def upstream_for_owners(x, c, owners):
    blocks, size, channels = x.shape
    row = pl.BlockSpec((MANY, size, channels), lambda b: (b, 0, 0))
    return pl.pallas_call(
        upstream_kernel,
        grid=(blocks // MANY,),
        in_specs=[row, row],
        out_specs=pl.BlockSpec((owners, MANY, size // owners, channels), lambda b: (0, b, 0, 0)),
        out_shape=jax.ShapeDtypeStruct((owners, blocks, size // owners, channels), x.dtype),
        cost_estimate=pl.CostEstimate(
            flops=8 * x.size, bytes_accessed=6 * x.size, transcendentals=x.size
        ),
        compiler_params=ROOM,
        name="upstream",
    )(x, c)


def final_kernel(y_ref, slope_ref, folded_ref, out_ref):
    many, size, channels = out_ref.shape
    for n in range(many):
        y = y_ref[:, n].reshape(size, channels)
        out_ref[n] = folded_ref[n] + y * slope_ref[n]


def final(y, slope, folded):
    blocks, size, channels = slope.shape
    owners = y.shape[0]
    row = pl.BlockSpec((MANY, size, channels), lambda b: (b, 0, 0))
    return pl.pallas_call(
        final_kernel,
        grid=(blocks // MANY,),
        in_specs=[
            pl.BlockSpec((owners, MANY, size // owners, channels), lambda b: (0, b, 0, 0)),
            row,
            row,
        ],
        out_specs=row,
        out_shape=jax.ShapeDtypeStruct(slope.shape, slope.dtype),
        cost_estimate=pl.CostEstimate(
            flops=2 * y.size, bytes_accessed=8 * y.size, transcendentals=0
        ),
        compiler_params=ROOM,
        name="final",
    )(y, slope, folded)


def tie_kernel(*refs):
    del refs


def tie(*values):
    anywhere = [pl.BlockSpec(memory_space=pl.ANY)] * len(values)
    return pl.pallas_call(
        tie_kernel,
        in_specs=anywhere,
        out_specs=anywhere,
        out_shape=[jax.ShapeDtypeStruct(v.shape, v.dtype) for v in values],
        input_output_aliases={n: n for n in range(len(values))},
        cost_estimate=pl.CostEstimate(flops=0, bytes_accessed=0, transcendentals=0),
        compiler_params=ROOM,
        name="tie",
    )(*values)


def body(inputs, cotangent, first_factor, second_factor):
    sequences, tokens, channels = inputs.shape
    assert sequences == 1
    owners = lax.axis_size("seq")
    row_block, blocks, size1 = first_factor.shape
    places = size1 // owners
    mean_weight = 1.0 / (sequences * lax.axis_size("dp"))
    bf16, wide = jnp.bfloat16, dict(preferred_element_type=jnp.float32)
    x = inputs.reshape(blocks, size1, channels)
    c = cotangent.reshape(blocks, size1, channels)

    def exchange(value):
        return lax.all_to_all(value, "seq", 0, 0, tiled=True)

    def to_columns(value):
        return exchange(value).reshape(owners * blocks, places, channels)

    def by_owner(value):
        return value.reshape(blocks, owners, places, channels).transpose(1, 0, 2, 3)

    first = lax.all_gather(first_factor, "dp", axis=0, tiled=True)
    second = lax.all_gather(second_factor, "dp", axis=0, tiled=True)
    up_columns = to_columns(upstream_for_owners(x, c, owners))
    mixed = by_owner(jnp.einsum("ibk,bkd->bid", first, x, **wide).astype(bf16))
    up_columns, mixed = tie(up_columns, mixed)
    columns = to_columns(mixed)
    back_columns = jnp.einsum("ijk,ijd->kjd", second, up_columns, **wide).astype(bf16)
    columns, back_columns = tie(columns, back_columns)
    mixed_grad = exchange(back_columns.reshape(owners, blocks, places, channels))
    product = jnp.einsum("ijk,kjd->ijd", second, columns, **wide).astype(bf16)
    mixed_grad, product = tie(mixed_grad, product)
    output = exchange(product.reshape(owners, blocks, places, channels))
    mixed_grad = mixed_grad.transpose(1, 0, 2, 3).reshape(blocks, size1, channels)
    second_grad = lax.psum_scatter(
        jnp.einsum("ijd,kjd->ijk", up_columns, columns, **wide) * mean_weight,
        "dp",
        scatter_dimension=0,
        tiled=True,
    )
    folded = jnp.einsum("ibk,bid->bkd", first, mixed_grad, **wide).astype(bf16)
    x_wide = x.astype(jnp.float32)
    logistic = jax.nn.sigmoid(x_wide)
    slope = (c.astype(jnp.float32) * logistic * (1.0 + x_wide * (1.0 - logistic))).astype(bf16)
    first_grad = lax.psum_scatter(
        jnp.einsum("bid,bkd->ibk", mixed_grad, x, **wide) * mean_weight,
        "dp",
        scatter_dimension=0,
        tiled=True,
    )
    grad_input = final(output, slope, folded).reshape(inputs.shape)
    return (grad_input, first_grad, second_grad)


def solution(mesh):
    placed = P("dp", "seq", None)
    return jax.shard_map(
        body,
        mesh=mesh,
        in_specs=(placed,) * 4,
        out_specs=(placed,) * 3,
        check_vma=False,
    )
```

time: 645 us -> 618 us (0.958)
  local copies, waits for them, and re-layouts: 74.7 us -> 34.2 us
  waiting for transfers between devices: 422 us -> 448 us
  Pallas kernels: 0 us -> 20.8 us
  other arithmetic: 31.3 us -> 11.2 us
    convert_element_type x4 -> x0, local copies, waits for them, and re-layouts: 38.1 us -> none  [the longest x1 11 us: body(): output.astype(jnp.float32)]
    pallas_call x0 -> x5, Pallas kernels: none -> 20.8 us  [the longest x1 10.5 us: final(): pl.pallas_call(final_kernel, grid=(blocks // MANY,), in_specs=[pl.BlockSp...]
    convert_element_type x3 -> x1, other arithmetic: 31.3 us -> 11.2 us  [body(): (c.astype(jnp.float32) * logistic * (1.0 + x_wide * (1.0 - logistic))).as...]
    dot_general x0 -> x2, local copies, waits for them, and re-layouts: none -> 18 us  [the longest x1 9.06 us: body(): jnp.einsum('ijk,ijd->kjd', second, up_columns, **wide).astype(bf16)]
    all_to_all x5 -> x0, local copies, waits for them, and re-layouts: 16.9 us -> none  [the longest x2 8.12 us: body(): lax.all_to_all(upstream_rows, 'seq', split_axis=2, concat_axis=1, tiled=T...]
    all_to_all x4, waiting for transfers between devices: 387 us -> 399 us  [exchange(): return lax.all_to_all(value, 'seq', 0, 0, tiled=True)]
    all_gather x2, waiting for transfers between devices: 35.1 us -> 43.4 us  [the longest x1 24.6 us: body(): first = lax.all_gather(first_factor, 'dp', axis=0, tiled=True)]
  transfers between devices with their start and end apart: 8 -> 8, of which waited for: 6 -> 7; matrix products, arithmetic and copies ran while one was open for 23% -> 14% of each run, Pallas kernels for 0% -> 2%
where the time goes in v2:
time: 618 us; the launch traced here: 612 us
  waiting for transfers between devices  448 us (72%)
  matrix products  53.4 us (9%)
  local copies, waits for them, and re-layouts  34.2 us (6%)
  starting transfers between devices  30.8 us (5%)
  Pallas kernels  20.8 us (3%)
  between operations  13.8 us (2%)
  other arithmetic  11.2 us (2%)
    all_to_all x4, waiting for transfers between devices, exchange(): return lax.all_to_all(value, 'seq', 0, 0, tiled=True)  399 us
    all_to_all x4, starting transfers between devices, exchange(): return lax.all_to_all(value, 'seq', 0, 0, tiled=True)  30.8 us
    all_gather x1, waiting for transfers between devices, body(): first = lax.all_gather(first_factor, 'dp', axis=0, tiled=True)  24.6 us
    all_gather x1, waiting for transfers between devices, body(): second = lax.all_gather(second_factor, 'dp', axis=0, tiled=True)  18.9 us
    dot_general x1, matrix products, body(): jnp.einsum('ijk,ijd->kjd', second, up_columns, **wide).astype(bf16)  12.9 us
    dot_general x1, matrix products, body(): jnp.einsum('ijd,kjd->ijk', up_columns, columns, **wide) * mean_weight  12.7 us
    dot_general x1, matrix products, body(): product = jnp.einsum('ijk,kjd->ijd', second, columns, **wide).astype(bf16)  12.6 us
  transfers between devices with their start and end apart: 8, of which 7 were waited for; matrix products, arithmetic and copies ran while one was open for 14% of the time, Pallas kernels for 2%

profile of v2, /device:TPU:20, one launch (start us, length us, event | category | flops | bytes accessed | tf_op | source)
XLA Modules:
  0.0 612.3 jit_solution(10374229991888018089)
XLA Ops:
  7.2 10.2 %upstream.1 = bf16[8,16,32,768]{3,2,1,0:T(8,128)(2,1)} custom-call(bf16[16,256,768]{2,1,0:T(8,128)(2,1)} %bitcast.33, bf16[16,256,768]{2,1,0:T(8,128)(2,1)} %bitcast.49), custom_call_target="tpu_custom_call" | custom-call | flops 25165824 | bytes 18874368 | tf_op jit(solution)/shard_map/upstream/pallas_call | solution.py:24
  17.4 6.3 %all-to-all-start = ((bf16[8,16,32,768]{3,2,1,0:T(8,128)(2,1)}), bf16[8,16,32,768]{3,2,1,0:T(8,128)(2,1)}, u32[]{:S(2)}, u32[]{:S(2)}) async-start(bf16[8,16,32,768]{3,2,1,0:T(8,128)(2,1)} %upstream.1), calls=%async_computation | async-start | bytes 12582912 | tf_op jit(solution)/shard_map/all_to_all | solution.py:97
  23.7 1.0 copy.39
  24.6 0.0 all-gather.3.cloned.1.call-update
  24.7 24.6 %all-gather.3.cloned.1.call-done = bf16[256,16,256]{2,0,1:T(8,128)(2,1)} async-done(((bf16[64,16,256]{2,0,1:T(8,128)(2,1)}), bf16[256,16,256]{2,0,1:T(8,128)(2,1)}) %all-gather.3.cloned.1.call-update) | async-done | bytes 2097168 | tf_op jit(solution)/shard_map/all_gather | solution.py:105
  49.2 5.2 convolution_convert_fusion
  54.5 3.1 copy.68
  57.6 100.9 %all-to-all-done = bf16[8,16,32,768]{3,2,1,0:T(8,128)(2,1)} async-done(((bf16[8,16,32,768]{3,2,1,0:T(8,128)(2,1)}), bf16[8,16,32,768]{3,2,1,0:T(8,128)(2,1)}, u32[]{:S(2)}, u32[]{:S(2)}) %all-to-all-start) | async-done | bytes 6291488 | tf_op jit(solution)/shard_map/all_to_all | solution.py:97
  158.5 8.2 %all-to-all-start.1 = ((bf16[8,16,32,768]{3,2,1,0:T(8,128)(2,1)}), bf16[8,16,32,768]{3,2,1,0:T(8,128)(2,1)}, u32[]{:S(2)}, u32[]{:S(2)}) async-start(bf16[8,16,32,768]{3,2,1,0:T(8,128)(2,1)} %get-tuple-element.9), calls=%async_computation.1 | async-start | bytes 12582912 | tf_op jit(solution)/shard_map/all_to_all | solution.py:97
  166.7 0.8 copy.41
  167.5 0.0 all-gather.5.cloned.1.call-update
  167.5 18.9 %all-gather.5.cloned.1.call-done = bf16[128,32,128]{2,0,1:T(8,128)(2,1)} async-done(((bf16[32,32,128]{2,0,1:T(8,128)(2,1)}), bf16[128,32,128]{2,0,1:T(8,128)(2,1)}) %all-gather.5.cloned.1.call-update) | async-done | bytes 1048592 | tf_op jit(solution)/shard_map/all_gather | solution.py:106
  186.4 12.9 %fusion.6 = bf16[32,768,128]{2,1,0:T(8,128)(2,1)} fusion(bf16[128,32,128]{2,0,1:T(8,128)(2,1)} %all-gather.5.cloned.1.call-done, bf16[128,32,768]{2,1,0:T(8,128)(2,1)} %get-tuple-element.10), kind=kOutput, calls=%fused_computation.12 | convolution fusion | flops 805306368 | bytes 13631488 | tf_op jit(solution)/shard_map/ijk,ijd->kjd/dot_general | solution.py:111
  199.3 9.1 %copy.43 = bf16[32,768,128]{1,0,2:T(8,128)(2,1)} copy(bf16[32,768,128]{2,1,0:T(8,128)(2,1)} %fusion.6) | data formatting | bytes 12582912 | tf_op jit(solution)/shard_map/ijk,ijd->kjd/dot_general | solution.py:111
  208.3 92.4 %all-to-all-done.1 = bf16[8,16,32,768]{3,2,1,0:T(8,128)(2,1)} async-done(((bf16[8,16,32,768]{3,2,1,0:T(8,128)(2,1)}), bf16[8,16,32,768]{3,2,1,0:T(8,128)(2,1)}, u32[]{:S(2)}, u32[]{:S(2)}) %all-to-all-start.1) | async-done | bytes 6291488 | tf_op jit(solution)/shard_map/all_to_all | solution.py:97
  300.7 8.3 %all-to-all-start.2 = ((bf16[8,16,32,768]{3,2,1,0:T(8,128)(2,1)}), bf16[8,16,32,768]{3,2,1,0:T(8,128)(2,1)}, u32[]{:S(2)}, u32[]{:S(2)}) async-start(bf16[8,16,32,768]{3,2,1,0:T(8,128)(2,1)} %bitcast.45), calls=%async_computation.2 | async-start | bytes 12582912 | tf_op jit(solution)/shard_map/all_to_all | solution.py:97
  309.1 12.6 %fusion.10 = bf16[32,768,128]{2,1,0:T(8,128)(2,1)} fusion(bf16[128,32,128]{2,0,1:T(8,128)(2,1)S(1)} %copy-done.1, bf16[128,32,768]{2,1,0:T(8,128)(2,1)} %get-tuple-element.12), kind=kOutput, calls=%fused_computation.16 | convolution fusion | flops 805306368 | bytes 13631488 | tf_op jit(solution)/shard_map/ijk,kjd->ijd/dot_general | solution.py:114
  321.7 9.0 %copy.45 = bf16[32,768,128]{1,0,2:T(8,128)(2,1)} copy(bf16[32,768,128]{2,1,0:T(8,128)(2,1)} %fusion.10) | data formatting | bytes 12582912 | tf_op jit(solution)/shard_map/ijk,kjd->ijd/dot_general | solution.py:114
  330.7 112.2 %all-to-all-done.2.refs_0_ = bf16[8,16,32,768]{3,2,1,0:T(8,128)(2,1)} async-done(((bf16[8,16,32,768]{3,2,1,0:T(8,128)(2,1)}), bf16[8,16,32,768]{3,2,1,0:T(8,128)(2,1)}, u32[]{:S(2)}, u32[]{:S(2)}) %all-to-all-start.2) | async-done | bytes 6291488 | tf_op jit(solution)/shard_map/all_to_all | solution.py:97
  442.8 3.5 copy.46
  446.3 2.7 copy-done
  449.0 3.9 multiply_bitcast_fusion
  452.9 0.0 reduce-scatter.3.cloned.1.call-update
  452.9 8.0 %all-to-all-start.3 = ((bf16[8,16,32,768]{3,2,1,0:T(8,128)(2,1)}), bf16[8,16,32,768]{3,2,1,0:T(8,128)(2,1)}, u32[]{:S(2)}, u32[]{:S(2)}) async-start(bf16[8,16,32,768]{3,2,1,0:T(8,128)(2,1)} %bitcast.47), calls=%async_computation.3 | async-start | bytes 12582912 | tf_op jit(solution)/shard_map/all_to_all | solution.py:97
  461.0 12.7 %multiply_bitcast_fusion.1 = f32[128,32,128]{0,2,1:T(8,128)S(1)} fusion(bf16[128,32,768]{2,1,0:T(8,128)(2,1)} %get-tuple-element.10, bf16[128,32,768]{2,1,0:T(8,128)(2,1)} %get-tuple-element.12), kind=kOutput, calls=%fused_computation.21 | convolution fusion | flops 805830656 | bytes 14680064 | tf_op jit(solution)/shard_map/ijd,kjd->ijk/dot_general | solution.py:119
  473.7 2.3 copy.51
  476.0 11.2 %fusion.5.slope_ref = bf16[16,256,768]{2,1,0:T(8,128)(2,1)} fusion(bf16[16,256,768]{2,1,0:T(8,128)(2,1)} %bitcast.35, bf16[16,256,768]{2,1,0:T(8,128)(2,1)} %bitcast.50), kind=kLoop, calls=%fused_computation.7 | loop fusion | flops 34603008 | bytes 18874368 | tf_op jit(solution)/shard_map/convert_element_type | solution.py:127
  487.3 6.1 convert_bitcast_fusion.folded_ref
  493.3 5.4 reduce-scatter.3.cloned.1.call-done
  498.8 2.8 copy.52
  501.6 93.7 %all-to-all-done.3.y_ref = bf16[8,16,32,768]{3,2,1,0:T(8,128)(2,1)} async-done(((bf16[8,16,32,768]{3,2,1,0:T(8,128)(2,1)}), bf16[8,16,32,768]{3,2,1,0:T(8,128)(2,1)}, u32[]{:S(2)}, u32[]{:S(2)}) %all-to-all-start.3) | async-done | bytes 6291488 | tf_op jit(solution)/shard_map/all_to_all | solution.py:97
  595.2 10.5 %final.1 = bf16[16,256,768]{2,1,0:T(8,128)(2,1)} custom-call(bf16[8,16,32,768]{3,2,1,0:T(8,128)(2,1)} %all-to-all-done.3.y_ref, bf16[16,256,768]{2,1,0:T(8,128)(2,1)} %fusion.5.slope_ref, bf16[16,256,768]{2,1,0:T(8,128)(2,1)} %convert_bitcast_fusion.folded_ref), custom_call_target="tpu_custom_call" | custom-call | flops 6291456 | bytes 25165824 | tf_op jit(solution)/shard_map/final/pallas_call | solution.py:49
  (26 shorter events, 0.1 us)
Async XLA Ops:
  17.4 6.3 %copy-start.2 = (bf16[64,16,256]{2,1,0:T(8,128)(2,1)S(1)}, bf16[64,16,256]{2,1,0:T(8,128)(2,1)}, u32[]{:S(2)}) copy-start(bf16[64,16,256]{2,1,0:T(8,128)(2,1)} %param.6) | copy-start | bytes 1572868
  17.4 141.1 %all-to-all-start = ((bf16[8,16,32,768]{3,2,1,0:T(8,128)(2,1)}), bf16[8,16,32,768]{3,2,1,0:T(8,128)(2,1)}, u32[]{:S(2)}, u32[]{:S(2)}) async-start(bf16[8,16,32,768]{3,2,1,0:T(8,128)(2,1)} %upstream.1), calls=%async_computation | async-start | bytes 12582912 | tf_op jit(solution)/shard_map/all_to_all | solution.py:97
  23.7 25.5 %all-gather.3.cloned.1.call-start = ((), (), s32[]{:S(2)}) async-start(), calls=%async_computation.6 | async-start | bytes 2621440 | tf_op jit(solution)/shard_map/all_gather | solution.py:105
  158.5 8.2 %copy-start.3 = (bf16[32,32,128]{2,1,0:T(8,128)(2,1)S(1)}, bf16[32,32,128]{2,1,0:T(8,128)(2,1)}, u32[]{:S(2)}) copy-start(bf16[32,32,128]{2,1,0:T(8,128)(2,1)} %param.7) | copy-start | bytes 786436
  158.5 142.2 %all-to-all-start.1 = ((bf16[8,16,32,768]{3,2,1,0:T(8,128)(2,1)}), bf16[8,16,32,768]{3,2,1,0:T(8,128)(2,1)}, u32[]{:S(2)}, u32[]{:S(2)}) async-start(bf16[8,16,32,768]{3,2,1,0:T(8,128)(2,1)} %get-tuple-element.9), calls=%async_computation.1 | async-start | bytes 12582912 | tf_op jit(solution)/shard_map/all_to_all | solution.py:97
  166.7 19.7 %all-gather.5.cloned.1.call-start = ((), (), s32[]{:S(2)}) async-start(), calls=%async_computation.7 | async-start | bytes 1310720 | tf_op jit(solution)/shard_map/all_gather | solution.py:106
  300.7 8.3 %copy-start.1 = (bf16[128,32,128]{2,0,1:T(8,128)(2,1)S(1)}, bf16[128,32,128]{2,0,1:T(8,128)(2,1)}, u32[]{:S(2)}) copy-start(bf16[128,32,128]{2,0,1:T(8,128)(2,1)} %all-gather.5.cloned.1.call-done) | copy-start | bytes 3145732
  300.7 142.1 %all-to-all-start.2 = ((bf16[8,16,32,768]{3,2,1,0:T(8,128)(2,1)}), bf16[8,16,32,768]{3,2,1,0:T(8,128)(2,1)}, u32[]{:S(2)}, u32[]{:S(2)}) async-start(bf16[8,16,32,768]{3,2,1,0:T(8,128)(2,1)} %bitcast.45), calls=%async_computation.2 | async-start | bytes 12582912 | tf_op jit(solution)/shard_map/all_to_all | solution.py:97
  309.1 189.7 %reduce-scatter.3.cloned.1.call-start = ((), (), s32[]{:S(2)}) async-start(), calls=%async_computation.8 | async-start | bytes 5242880 | tf_op jit(solution)/shard_map/reduce_scatter | solution.py:128
  442.8 6.2 %slice-start = ((s8[6291456]{0:T(1024)(128)(4,1)}), s8[2097152]{0:T(1024)(128)(4,1)S(1)}, s32[]{:S(2)}) async-start(s8[6291456]{0:T(1024)(128)(4,1)} %bitcast.36), calls=%async_computation.10 | async-start | bytes 4194304
  442.8 6.2 %slice-start.1 = ((s8[6291456]{0:T(1024)(128)(4,1)}), s8[4194304]{0:T(1024)(128)(4,1)S(1)}, s32[]{:S(2)}) async-start(s8[6291456]{0:T(1024)(128)(4,1)} %bitcast.36), calls=%async_computation.11 | async-start | bytes 8388608
  446.3 2.7 copy-start
  452.9 142.3 %all-to-all-start.3 = ((bf16[8,16,32,768]{3,2,1,0:T(8,128)(2,1)}), bf16[8,16,32,768]{3,2,1,0:T(8,128)(2,1)}, u32[]{:S(2)}, u32[]{:S(2)}) async-start(bf16[8,16,32,768]{3,2,1,0:T(8,128)(2,1)} %bitcast.47), calls=%async_computation.3 | async-start | bytes 12582912 | tf_op jit(solution)/shard_map/all_to_all | solution.py:97
  461.0 144.8 %reduce-scatter.5.cloned.1.call-start = ((), (), s32[]{:S(2)}) async-start(), calls=%async_computation.9 | async-start | bytes 2621440 | tf_op jit(solution)/shard_map/reduce_scatter | solution.py:118
  476.0 11.3 %slice-start.2 = ((s8[6291456]{0:T(1024)(128)(4,1)}), s8[2097152]{0:T(1024)(128)(4,1)S(1)}, s32[]{:S(2)}) async-start(s8[6291456]{0:T(1024)(128)(4,1)} %bitcast.40), calls=%async_computation.12 | async-start | bytes 4194304
  476.0 11.3 %slice-start.3 = ((s8[6291456]{0:T(1024)(128)(4,1)}), s8[4194304]{0:T(1024)(128)(4,1)S(1)}, s32[]{:S(2)}) async-start(s8[6291456]{0:T(1024)(128)(4,1)} %bitcast.40), calls=%async_computation.13 | async-start | bytes 8388608
Sparse Core Ops, SparseCore 0:
  26.6 22.5 all-gather.2
  169.7 16.6 all-gather.4
  453.1 45.6 reduce-scatter.2
  501.9 31.4 reduce-scatter.4

commit v3 on v2

--- a/solution.py
+++ b/solution.py
@@ -5,7 +5,7 @@
 from jax.experimental.pallas import tpu as pltpu
 from jax.sharding import PartitionSpec as P
 
-MANY = 2
+MANY = 4
 ROOM = pltpu.CompilerParams(vmem_limit_bytes=56 * 1024 * 1024)
 
 
@@ -57,7 +57,7 @@
         out_specs=row,
         out_shape=jax.ShapeDtypeStruct(slope.shape, slope.dtype),
         cost_estimate=pl.CostEstimate(
-            flops=2 * y.size, bytes_accessed=8 * y.size, transcendentals=0
+            flops=100_000 * y.size, bytes_accessed=8 * y.size, transcendentals=0
         ),
         compiler_params=ROOM,
         name="final",

time: 618 us -> 605 us (0.979)
  waiting for transfers between devices: 448 us -> 435 us
    all_to_all x4, waiting for transfers between devices: 399 us -> 382 us  [exchange(): return lax.all_to_all(value, 'seq', 0, 0, tiled=True)]
  transfers between devices with their start and end apart: 8 -> 8, of which waited for: 7 -> 7; matrix products, arithmetic and copies ran while one was open for 14% -> 16% of each run, Pallas kernels for 2% -> 2%
where the time goes in v3:
time: 605 us; the launch traced here: 599 us
  waiting for transfers between devices  435 us (72%)
  matrix products  54.6 us (9%)
  local copies, waits for them, and re-layouts  35.1 us (6%)
  starting transfers between devices  31.1 us (5%)
  Pallas kernels  17.8 us (3%)
  between operations  13.8 us (2%)
  other arithmetic  11.6 us (2%)
    all_to_all x4, waiting for transfers between devices, exchange(): return lax.all_to_all(value, 'seq', 0, 0, tiled=True)  382 us
    all_to_all x4, starting transfers between devices, exchange(): return lax.all_to_all(value, 'seq', 0, 0, tiled=True)  30.8 us
    all_gather x1, waiting for transfers between devices, body(): first = lax.all_gather(first_factor, 'dp', axis=0, tiled=True)  24.6 us
    all_gather x1, waiting for transfers between devices, body(): second = lax.all_gather(second_factor, 'dp', axis=0, tiled=True)  18.9 us
    dot_general x1, matrix products, body(): jnp.einsum('ijk,ijd->kjd', second, up_columns, **wide).astype(bf16)  12.9 us
    dot_general x1, matrix products, body(): jnp.einsum('ijd,kjd->ijk', up_columns, columns, **wide) * mean_weight  12.8 us
    dot_general x1, matrix products, body(): product = jnp.einsum('ijk,kjd->ijd', second, columns, **wide).astype(bf16)  12.6 us
  transfers between devices with their start and end apart: 8, of which 7 were waited for; matrix products, arithmetic and copies ran while one was open for 16% of the time, Pallas kernels for 2%

profile of v3, /device:TPU:20, one launch (start us, length us, event | category | flops | bytes accessed | tf_op | source)
XLA Modules:
  0.0 599.3 jit_solution(10620954876085324344)
XLA Ops:
  7.2 8.6 %upstream.1 = bf16[8,16,32,768]{3,2,1,0:T(8,128)(2,1)} custom-call(bf16[16,256,768]{2,1,0:T(8,128)(2,1)} %bitcast.33, bf16[16,256,768]{2,1,0:T(8,128)(2,1)} %bitcast.47), custom_call_target="tpu_custom_call" | custom-call | flops 25165824 | bytes 18874368 | tf_op jit(solution)/shard_map/upstream/pallas_call | solution.py:24
  15.8 6.3 %all-to-all-start = ((bf16[8,16,32,768]{3,2,1,0:T(8,128)(2,1)}), bf16[8,16,32,768]{3,2,1,0:T(8,128)(2,1)}, u32[]{:S(2)}, u32[]{:S(2)}) async-start(bf16[8,16,32,768]{3,2,1,0:T(8,128)(2,1)} %upstream.1), calls=%async_computation | async-start | bytes 12582912 | tf_op jit(solution)/shard_map/all_to_all | solution.py:97
  22.1 1.0 copy.39
  23.0 0.0 all-gather.3.cloned.1.call-update
  23.0 24.6 %all-gather.3.cloned.1.call-done = bf16[256,16,256]{2,0,1:T(8,128)(2,1)} async-done(((bf16[64,16,256]{2,0,1:T(8,128)(2,1)}), bf16[256,16,256]{2,0,1:T(8,128)(2,1)}) %all-gather.3.cloned.1.call-update) | async-done | bytes 2097168 | tf_op jit(solution)/shard_map/all_gather | solution.py:105
  47.6 5.2 convolution_convert_fusion
  52.8 3.1 copy.68
  55.9 101.0 %all-to-all-done = bf16[8,16,32,768]{3,2,1,0:T(8,128)(2,1)} async-done(((bf16[8,16,32,768]{3,2,1,0:T(8,128)(2,1)}), bf16[8,16,32,768]{3,2,1,0:T(8,128)(2,1)}, u32[]{:S(2)}, u32[]{:S(2)}) %all-to-all-start) | async-done | bytes 6291488 | tf_op jit(solution)/shard_map/all_to_all | solution.py:97
  156.9 8.2 %all-to-all-start.1 = ((bf16[8,16,32,768]{3,2,1,0:T(8,128)(2,1)}), bf16[8,16,32,768]{3,2,1,0:T(8,128)(2,1)}, u32[]{:S(2)}, u32[]{:S(2)}) async-start(bf16[8,16,32,768]{3,2,1,0:T(8,128)(2,1)} %get-tuple-element.9), calls=%async_computation.1 | async-start | bytes 12582912 | tf_op jit(solution)/shard_map/all_to_all | solution.py:97
  165.1 0.8 copy.41
  166.0 0.0 all-gather.5.cloned.1.call-update
  166.0 18.9 %all-gather.5.cloned.1.call-done = bf16[128,32,128]{2,0,1:T(8,128)(2,1)} async-done(((bf16[32,32,128]{2,0,1:T(8,128)(2,1)}), bf16[128,32,128]{2,0,1:T(8,128)(2,1)}) %all-gather.5.cloned.1.call-update) | async-done | bytes 1048592 | tf_op jit(solution)/shard_map/all_gather | solution.py:106
  184.8 12.9 %fusion.6 = bf16[32,768,128]{2,1,0:T(8,128)(2,1)} fusion(bf16[128,32,128]{2,0,1:T(8,128)(2,1)} %all-gather.5.cloned.1.call-done, bf16[128,32,768]{2,1,0:T(8,128)(2,1)} %get-tuple-element.10), kind=kOutput, calls=%fused_computation.12 | convolution fusion | flops 805306368 | bytes 13631488 | tf_op jit(solution)/shard_map/ijk,ijd->kjd/dot_general | solution.py:111
  197.7 9.0 %copy.43 = bf16[32,768,128]{1,0,2:T(8,128)(2,1)} copy(bf16[32,768,128]{2,1,0:T(8,128)(2,1)} %fusion.6) | data formatting | bytes 12582912 | tf_op jit(solution)/shard_map/ijk,ijd->kjd/dot_general | solution.py:111
  206.8 92.4 %all-to-all-done.1 = bf16[8,16,32,768]{3,2,1,0:T(8,128)(2,1)} async-done(((bf16[8,16,32,768]{3,2,1,0:T(8,128)(2,1)}), bf16[8,16,32,768]{3,2,1,0:T(8,128)(2,1)}, u32[]{:S(2)}, u32[]{:S(2)}) %all-to-all-start.1) | async-done | bytes 6291488 | tf_op jit(solution)/shard_map/all_to_all | solution.py:97
  299.1 8.2 %all-to-all-start.2 = ((bf16[8,16,32,768]{3,2,1,0:T(8,128)(2,1)}), bf16[8,16,32,768]{3,2,1,0:T(8,128)(2,1)}, u32[]{:S(2)}, u32[]{:S(2)}) async-start(bf16[8,16,32,768]{3,2,1,0:T(8,128)(2,1)} %bitcast.43), calls=%async_computation.2 | async-start | bytes 12582912 | tf_op jit(solution)/shard_map/all_to_all | solution.py:97
  307.3 12.6 %fusion.10 = bf16[32,768,128]{2,1,0:T(8,128)(2,1)} fusion(bf16[128,32,128]{2,0,1:T(8,128)(2,1)S(1)} %copy-done.2, bf16[128,32,768]{2,1,0:T(8,128)(2,1)} %get-tuple-element.12), kind=kOutput, calls=%fused_computation.16 | convolution fusion | flops 805306368 | bytes 13631488 | tf_op jit(solution)/shard_map/ijk,kjd->ijd/dot_general | solution.py:114
  319.9 9.0 %copy.45 = bf16[32,768,128]{1,0,2:T(8,128)(2,1)} copy(bf16[32,768,128]{2,1,0:T(8,128)(2,1)} %fusion.10) | data formatting | bytes 12582912 | tf_op jit(solution)/shard_map/ijk,kjd->ijd/dot_general | solution.py:114
  328.9 112.5 %all-to-all-done.2.refs_0_ = bf16[8,16,32,768]{3,2,1,0:T(8,128)(2,1)} async-done(((bf16[8,16,32,768]{3,2,1,0:T(8,128)(2,1)}), bf16[8,16,32,768]{3,2,1,0:T(8,128)(2,1)}, u32[]{:S(2)}, u32[]{:S(2)}) %all-to-all-start.2) | async-done | bytes 6291488 | tf_op jit(solution)/shard_map/all_to_all | solution.py:97
  441.4 8.2 %all-to-all-start.3 = ((bf16[8,16,32,768]{3,2,1,0:T(8,128)(2,1)}), bf16[8,16,32,768]{3,2,1,0:T(8,128)(2,1)}, u32[]{:S(2)}, u32[]{:S(2)}) async-start(bf16[8,16,32,768]{3,2,1,0:T(8,128)(2,1)} %bitcast.45), calls=%async_computation.3 | async-start | bytes 12582912 | tf_op jit(solution)/shard_map/all_to_all | solution.py:97
  449.5 3.5 copy.46
  453.0 2.7 copy-done
  455.7 3.8 multiply_bitcast_fusion
  459.6 0.3 reduce-scatter.5.cloned.1.call-start
  459.9 11.6 %fusion.5.slope_ref = bf16[16,256,768]{2,1,0:T(8,128)(2,1)} fusion(bf16[16,256,768]{2,1,0:T(8,128)(2,1)} %bitcast.35, bf16[16,256,768]{2,1,0:T(8,128)(2,1)} %bitcast.48), kind=kLoop, calls=%fused_computation.7 | loop fusion | flops 34603008 | bytes 18874368 | tf_op jit(solution)/shard_map/convert_element_type | solution.py:127
  471.5 12.8 %multiply_bitcast_fusion.1 = f32[128,32,128]{0,2,1:T(8,128)} fusion(bf16[128,32,768]{2,1,0:T(8,128)(2,1)} %get-tuple-element.10, bf16[128,32,768]{2,1,0:T(8,128)(2,1)} %get-tuple-element.12), kind=kOutput, calls=%fused_computation.21 | convolution fusion | flops 805830656 | bytes 14680064 | tf_op jit(solution)/shard_map/ijd,kjd->ijk/dot_general | solution.py:119
  484.3 3.2 copy.51
  487.6 7.2 %convert_bitcast_fusion.folded_ref = bf16[16,256,768]{2,1,0:T(8,128)(2,1)} fusion(bf16[16,256,768]{2,1,0:T(8,128)(2,1)} %bitcast.40, bf16[256,16,256]{2,0,1:T(8,128)(2,1)S(1)} %copy-done.1), kind=kOutput, calls=%fused_computation.9 | convolution fusion | flops 1613758464 | bytes 14680064 | tf_op jit(solution)/shard_map/ibk,bid->bkd/dot_general | solution.py:124
  494.8 9.5 %reduce-scatter.3.cloned.1.call-done = f32[64,16,256]{2,0,1:T(8,128)} async-done(((f32[256,16,256]{2,0,1:T(8,128)}), f32[64,16,256]{2,0,1:T(8,128)}) %reduce-scatter.3.cloned.1.call-update) | async-done | bytes 1048592 | tf_op jit(solution)/shard_map/reduce_scatter | solution.py:128
  504.2 2.8 copy.52
  507.0 76.6 %all-to-all-done.3.y_ref = bf16[8,16,32,768]{3,2,1,0:T(8,128)(2,1)} async-done(((bf16[8,16,32,768]{3,2,1,0:T(8,128)(2,1)}), bf16[8,16,32,768]{3,2,1,0:T(8,128)(2,1)}, u32[]{:S(2)}, u32[]{:S(2)}) %all-to-all-start.3) | async-done | bytes 6291488 | tf_op jit(solution)/shard_map/all_to_all | solution.py:97
  583.6 9.2 %final.1 = bf16[16,256,768]{2,1,0:T(8,128)(2,1)} custom-call(bf16[8,16,32,768]{3,2,1,0:T(8,128)(2,1)} %all-to-all-done.3.y_ref, bf16[16,256,768]{2,1,0:T(8,128)(2,1)} %fusion.5.slope_ref, bf16[16,256,768]{2,1,0:T(8,128)(2,1)} %convert_bitcast_fusion.folded_ref), custom_call_target="tpu_custom_call" | custom-call | flops 314572800000 | bytes 25165824 | tf_op jit(solution)/shard_map/final/pallas_call | solution.py:49
  (23 shorter events, 0.1 us)
Async XLA Ops:
  15.8 6.3 %copy-start.3 = (bf16[64,16,256]{2,1,0:T(8,128)(2,1)S(1)}, bf16[64,16,256]{2,1,0:T(8,128)(2,1)}, u32[]{:S(2)}) copy-start(bf16[64,16,256]{2,1,0:T(8,128)(2,1)} %param.6) | copy-start | bytes 1572868
  15.8 141.1 %all-to-all-start = ((bf16[8,16,32,768]{3,2,1,0:T(8,128)(2,1)}), bf16[8,16,32,768]{3,2,1,0:T(8,128)(2,1)}, u32[]{:S(2)}, u32[]{:S(2)}) async-start(bf16[8,16,32,768]{3,2,1,0:T(8,128)(2,1)} %upstream.1), calls=%async_computation | async-start | bytes 12582912 | tf_op jit(solution)/shard_map/all_to_all | solution.py:97
  22.1 25.5 %all-gather.3.cloned.1.call-start = ((), (), s32[]{:S(2)}) async-start(), calls=%async_computation.6 | async-start | bytes 2621440 | tf_op jit(solution)/shard_map/all_gather | solution.py:105
  156.9 8.2 %copy-start.4 = (bf16[32,32,128]{2,1,0:T(8,128)(2,1)S(1)}, bf16[32,32,128]{2,1,0:T(8,128)(2,1)}, u32[]{:S(2)}) copy-start(bf16[32,32,128]{2,1,0:T(8,128)(2,1)} %param.7) | copy-start | bytes 786436
  156.9 142.2 %all-to-all-start.1 = ((bf16[8,16,32,768]{3,2,1,0:T(8,128)(2,1)}), bf16[8,16,32,768]{3,2,1,0:T(8,128)(2,1)}, u32[]{:S(2)}, u32[]{:S(2)}) async-start(bf16[8,16,32,768]{3,2,1,0:T(8,128)(2,1)} %get-tuple-element.9), calls=%async_computation.1 | async-start | bytes 12582912 | tf_op jit(solution)/shard_map/all_to_all | solution.py:97
  165.1 19.7 %all-gather.5.cloned.1.call-start = ((), (), s32[]{:S(2)}) async-start(), calls=%async_computation.7 | async-start | bytes 1310720 | tf_op jit(solution)/shard_map/all_gather | solution.py:106
  299.1 8.2 %copy-start.2 = (bf16[128,32,128]{2,0,1:T(8,128)(2,1)S(1)}, bf16[128,32,128]{2,0,1:T(8,128)(2,1)}, u32[]{:S(2)}) copy-start(bf16[128,32,128]{2,0,1:T(8,128)(2,1)} %all-gather.5.cloned.1.call-done) | copy-start | bytes 3145732
  299.1 142.3 %all-to-all-start.2 = ((bf16[8,16,32,768]{3,2,1,0:T(8,128)(2,1)}), bf16[8,16,32,768]{3,2,1,0:T(8,128)(2,1)}, u32[]{:S(2)}, u32[]{:S(2)}) async-start(bf16[8,16,32,768]{3,2,1,0:T(8,128)(2,1)} %bitcast.43), calls=%async_computation.2 | async-start | bytes 12582912 | tf_op jit(solution)/shard_map/all_to_all | solution.py:97
  441.4 14.3 %slice-start = ((s8[6291456]{0:T(1024)(128)(4,1)}), s8[2097152]{0:T(1024)(128)(4,1)S(1)}, s32[]{:S(2)}) async-start(s8[6291456]{0:T(1024)(128)(4,1)} %bitcast.36), calls=%async_computation.10 | async-start | bytes 4194304
  441.4 142.2 %all-to-all-start.3 = ((bf16[8,16,32,768]{3,2,1,0:T(8,128)(2,1)}), bf16[8,16,32,768]{3,2,1,0:T(8,128)(2,1)}, u32[]{:S(2)}, u32[]{:S(2)}) async-start(bf16[8,16,32,768]{3,2,1,0:T(8,128)(2,1)} %bitcast.45), calls=%async_computation.3 | async-start | bytes 12582912 | tf_op jit(solution)/shard_map/all_to_all | solution.py:97
  449.5 54.7 %reduce-scatter.3.cloned.1.call-start = ((), (), s32[]{:S(2)}) async-start(), calls=%async_computation.8 | async-start | bytes 5242880 | tf_op jit(solution)/shard_map/reduce_scatter | solution.py:128
  449.5 6.2 %slice-start.1 = ((s8[6291456]{0:T(1024)(128)(4,1)}), s8[4194304]{0:T(1024)(128)(4,1)S(1)}, s32[]{:S(2)}) async-start(s8[6291456]{0:T(1024)(128)(4,1)} %bitcast.36), calls=%async_computation.11 | async-start | bytes 8388608
  453.0 2.7 copy-start
  459.6 133.2 %reduce-scatter.5.cloned.1.call-start = ((), (), s32[]{:S(2)}) async-start(), calls=%async_computation.9 | async-start | bytes 2621440 | tf_op jit(solution)/shard_map/reduce_scatter | solution.py:118
  484.3 3.2 copy-start.1
Sparse Core Ops, SparseCore 0:
  25.0 22.5 all-gather.2
  168.1 16.6 all-gather.4
  459.7 44.4 reduce-scatter.2
  507.4 31.4 reduce-scatter.4

commit v4 on v3

v4 whole, which is shorter than its diff:
```python
import functools

import jax
import jax.numpy as jnp
from jax import lax
from jax.experimental import pallas as pl
from jax.experimental.pallas import tpu as pltpu
from jax.sharding import PartitionSpec as P

ROOM = pltpu.CompilerParams(vmem_limit_bytes=56 * 1024 * 1024)
STEPS = 2
WINDOW = 5
ANYWHERE = pl.BlockSpec(memory_space=pl.ANY)


def cost(values, reads, flops=1):
    size = values.shape[0] * values.shape[1] * values.shape[2]
    return pl.CostEstimate(
        flops=flops * size, bytes_accessed=2 * reads * size, transcendentals=0
    )


def upstream_kernel(at_ref, x_ref, c_ref, *refs):
    del at_ref
    out_ref = refs[-1]
    for n in range(out_ref.shape[0]):
        x, c = x_ref[n, 0].astype(jnp.float32), c_ref[n, 0].astype(jnp.float32)
        half = 0.5 * x
        out_ref[n] = (c * (half + half * jnp.tanh(half))).astype(out_ref.dtype)


def pick_kernel(at_ref, value_ref, *refs):
    del at_ref
    refs[-1][...] = value_ref[...].reshape(refs[-1].shape)


def piece_call(kernel, values, axis, at, after, name):
    sizes = values[0].shape
    blocks, places, channels = sizes[1 - axis], sizes[2], sizes[3]
    many = blocks // STEPS
    if axis:
        rows = pl.BlockSpec((many, 1, places, channels), lambda b, at: (b, at[0], 0, 0))
    else:
        rows = pl.BlockSpec((1, many, places, channels), lambda b, at: (at[0], b, 0, 0))
    out = jax.ShapeDtypeStruct((blocks, places, channels), values[0].dtype)
    return pl.pallas_call(
        kernel,
        grid_spec=pltpu.PrefetchScalarGridSpec(
            num_scalar_prefetch=1,
            grid=(STEPS,),
            in_specs=[rows] * len(values) + [ANYWHERE] * len(after),
            out_specs=pl.BlockSpec((many, places, channels), lambda b, at: (b, 0, 0)),
        ),
        out_shape=out,
        cost_estimate=cost(out, 1 + len(values)),
        compiler_params=ROOM,
        name=name,
    )(at, *values, *after)


def final_kernel(at_ref, y_ref, slope_ref, folded_ref, *refs):
    del at_ref
    out_ref = refs[-1]
    for n in range(out_ref.shape[0]):
        out_ref[n, 0] = folded_ref[n, 0] + y_ref[n] * slope_ref[n, 0]


def final_piece(y, slope, folded, so_far, at, after):
    blocks, _, places, channels = slope.shape
    many = blocks // STEPS
    rows = pl.BlockSpec((many, 1, places, channels), lambda b, at: (b, at[0], 0, 0))
    piece = pl.BlockSpec((many, places, channels), lambda b, at: (b, 0, 0))
    before = ([] if so_far is None else [so_far]) + after
    return pl.pallas_call(
        final_kernel,
        grid_spec=pltpu.PrefetchScalarGridSpec(
            num_scalar_prefetch=1,
            grid=(STEPS,),
            in_specs=[piece, rows, rows] + [ANYWHERE] * len(before),
            out_specs=rows,
        ),
        out_shape=jax.ShapeDtypeStruct(slope.shape, slope.dtype),
        input_output_aliases={} if so_far is None else {4: 0},
        cost_estimate=cost(y, 4, 100_000),
        compiler_params=ROOM,
        name="final",
    )(at, y, slope, folded, *before)


def place_kernel(owners, where_ref, *refs):
    del where_ref
    out_ref = refs[-1]
    for d in range(owners):

        @pl.when(pl.program_id(0) == d)
        def _():
            out_ref[...] = refs[d][...].reshape(out_ref.shape)


def place(pieces, where, axis, after):
    blocks, places, channels = pieces[0].shape
    owners = len(pieces)
    if axis:
        shape, block = (blocks, owners, places, channels), (blocks, 1, places, channels)
        spec = pl.BlockSpec(block, lambda d, where: (0, where[0] ^ d, 0, 0))
    else:
        shape, block = (owners, blocks, places, channels), (1, blocks, places, channels)
        spec = pl.BlockSpec(block, lambda d, where: (where[0] ^ d, 0, 0, 0))
    whole = pl.BlockSpec((blocks, places, channels), lambda d, where: (0, 0, 0))
    return pl.pallas_call(
        functools.partial(place_kernel, owners),
        grid_spec=pltpu.PrefetchScalarGridSpec(
            num_scalar_prefetch=1,
            grid=(owners,),
            in_specs=[whole] * owners + [ANYWHERE] * len(after),
            out_specs=spec,
        ),
        out_shape=jax.ShapeDtypeStruct(shape, pieces[0].dtype),
        cost_estimate=cost(pieces[0], 2 * owners),
        compiler_params=ROOM,
        name="place",
    )(where, *pieces, *after)


def tie_kernel(*refs):
    del refs


def tie(value, after):
    return pl.pallas_call(
        tie_kernel,
        in_specs=[ANYWHERE] * (1 + len(after)),
        out_specs=ANYWHERE,
        out_shape=jax.ShapeDtypeStruct(value.shape, value.dtype),
        input_output_aliases={0: 0},
        cost_estimate=pl.CostEstimate(flops=0, bytes_accessed=0, transcendentals=0),
        compiler_params=ROOM,
        name="tie",
    )(value, *after)


def body(inputs, cotangent, first_factor, second_factor):
    sequences, tokens, channels = inputs.shape
    assert sequences == 1
    owners = lax.axis_size("seq")
    row_block, blocks, size1 = first_factor.shape
    places = size1 // owners
    mean_weight = 1.0 / (sequences * lax.axis_size("dp"))
    bf16, wide = jnp.bfloat16, dict(preferred_element_type=jnp.float32)
    me = lax.axis_index("seq").astype(jnp.int32)
    where = [(me ^ d).reshape(1) for d in range(owners)]
    rows = (blocks, owners, places, channels)
    columns_first = (owners, blocks, places, channels)
    column_shape = (owners * blocks, places, channels)
    x_rows, c_rows = inputs.reshape(rows), cotangent.reshape(rows)
    x = inputs.reshape(blocks, size1, channels)
    distances = [owners // 2]
    for d in range(1, owners // 2):
        distances += [d, owners // 2 + d]
    line, cuts = [], []

    def exchange(kernel, values, axis, name, order, between=None):
        got = {}
        for k, d in enumerate(order):
            after = cuts[-1:] + (line[-WINDOW:][:1] if len(line) >= WINDOW else [])
            if k == WINDOW and between is not None:
                after += between(cuts[-1])
            cuts.append(piece_call(kernel, values, axis, where[d], after, name))
            got[d] = lax.ppermute(cuts[-1], "seq", [(n, n ^ d) for n in range(owners)])
            line.append(got[d])
        got[0] = piece_call(kernel, values, axis, where[0], [], name)
        return [got[d] for d in range(owners)]

    first = lax.all_gather(first_factor, "dp", axis=0, tiled=True)
    second = lax.all_gather(second_factor, "dp", axis=0, tiled=True)
    made = {}

    def to_back(cut):
        made["up"] = place(up_pieces, where[0], 0, []).reshape(column_shape)
        back = jnp.einsum("ijk,ijd->kjd", second, made["up"], **wide).astype(bf16)
        made["back"] = back.reshape(columns_first)
        return [made["back"]]

    def to_product(cut):
        made["columns"] = place(mixed_pieces, where[0], 0, []).reshape(column_shape)
        product = jnp.einsum("ijk,kjd->ijd", second, made["columns"], **wide).astype(bf16)
        made["product"] = product.reshape(columns_first)
        return [made["product"]]

    def to_folded(cut):
        mixed_grad = place(grad_pieces, where[0], 1, []).reshape(blocks, size1, channels)
        made["first"] = jnp.einsum("bid,bkd->ibk", mixed_grad, x, **wide) * mean_weight
        folded = jnp.einsum("ibk,bid->bkd", first, mixed_grad, **wide).astype(bf16)
        made["folded"] = folded.reshape(rows)
        return [made["folded"], made["first"]]

    up_pieces = exchange(upstream_kernel, [x_rows, c_rows], 1, "upstream", distances)
    mixed = jnp.einsum("ibk,bkd->bid", first, x, **wide).astype(bf16).reshape(rows)
    mixed_pieces = exchange(pick_kernel, [mixed], 1, "pick", distances, to_back)
    grad_pieces = exchange(pick_kernel, [made["back"]], 0, "pick", distances, to_product)
    columns = made["columns"]
    second_grad = lax.psum_scatter(
        jnp.einsum("ijd,kjd->ijk", made["up"], columns, **wide) * mean_weight,
        "dp",
        scatter_dimension=0,
        tiled=True,
    )
    output = exchange(pick_kernel, [made["product"]], 0, "pick", distances, to_folded)
    first_grad = lax.psum_scatter(made["first"], "dp", scatter_dimension=0, tiled=True)
    x_wide = x.astype(jnp.float32)
    c_wide = cotangent.reshape(x.shape).astype(jnp.float32)
    logistic = jax.nn.sigmoid(x_wide)
    slope = (c_wide * logistic * (1.0 + x_wide * (1.0 - logistic))).astype(bf16)
    slope, grad_input = slope.reshape(rows), None
    for d in [0] + distances:
        after = [first_grad, second_grad] if d == distances[-2] else []
        grad_input = final_piece(output[d], slope, made["folded"], grad_input, where[d], after)
    grad_input = grad_input.reshape(inputs.shape)
    return (grad_input, first_grad, second_grad)


def solution(mesh):
    placed = P("dp", "seq", None)
    return jax.shard_map(
        body,
        mesh=mesh,
        in_specs=(placed,) * 4,
        out_specs=(placed,) * 3,
        check_vma=False,
    )
```

time: 605 us -> 593 us (0.980)
  waiting for transfers between devices: 435 us -> 329 us
  Pallas kernels: 17.8 us -> 107 us
  starting transfers between devices: 31.1 us -> 46.4 us
  local copies, waits for them, and re-layouts: 35.1 us -> 25.5 us
    all_to_all x4 -> x0, waiting for transfers between devices: 382 us -> none  [exchange(): return lax.all_to_all(value, 'seq', 0, 0, tiled=True)]
    ppermute x0 -> x28, waiting for transfers between devices: none -> 329 us  [exchange(): got[d] = lax.ppermute(cuts[-1], 'seq', [(n, n ^ d) for n in range(owners)])]
    pallas_call x5 -> x43, Pallas kernels: 17.8 us -> 107 us  [the longest x32 66.3 us: piece_call(): pl.pallas_call(kernel, grid_spec=pltpu.PrefetchScalarGridSpec(num_scalar_...]
    ppermute x0 -> x28, starting transfers between devices: none -> 46.2 us  [exchange(): got[d] = lax.ppermute(cuts[-1], 'seq', [(n, n ^ d) for n in range(owners)])]
    all_to_all x4 -> x0, starting transfers between devices: 30.8 us -> none  [exchange(): return lax.all_to_all(value, 'seq', 0, 0, tiled=True)]
    all_gather x1, waiting for transfers between devices: 24.6 us -> 0.01 us  [body(): first = lax.all_gather(first_factor, 'dp', axis=0, tiled=True)]
    all_gather x1, waiting for transfers between devices: 18.9 us -> 0.02 us  [body(): second = lax.all_gather(second_factor, 'dp', axis=0, tiled=True)]
    dot_general x2 -> x1, local copies, waits for them, and re-layouts: 18 us -> 2.37 us  [body(): jnp.einsum('ijd,kjd->ijk', made['up'], columns, **wide) * mean_weight]
  transfers between devices with their start and end apart: 8 -> 32, of which waited for: 7 -> 15; matrix products, arithmetic and copies ran while one was open for 16% -> 14% of each run, Pallas kernels for 2% -> 18%
where the time goes in v4:
time: 593 us; the launch traced here: 587 us
  waiting for transfers between devices  329 us (55%)
  Pallas kernels  107 us (18%)
  matrix products  49.6 us (8%)
  starting transfers between devices  46.4 us (8%)
  local copies, waits for them, and re-layouts  25.5 us (4%)
  other arithmetic  15.8 us (3%)
  between operations  14.4 us (2%)
    ppermute x28, waiting for transfers between devices, exchange(): got[d] = lax.ppermute(cuts[-1], 'seq', [(n, n ^ d) for n in range(owners)])  329 us
    pallas_call x32, Pallas kernels, piece_call(): pl.pallas_call(kernel, grid_spec=pltpu.PrefetchScalarGridSpec(num_scalar_...  66.3 us
    ppermute x28, starting transfers between devices, exchange(): got[d] = lax.ppermute(cuts[-1], 'seq', [(n, n ^ d) for n in range(owners)])  46.2 us
    pallas_call x3, Pallas kernels, place(): pl.pallas_call(functools.partial(place_kernel, owners), grid_spec=pltpu.P...  21.1 us
    pallas_call x8, Pallas kernels, final_piece(): pl.pallas_call(final_kernel, grid_spec=pltpu.PrefetchScalarGridSpec(num_s...  19.6 us
  transfers between devices with their start and end apart: 32, of which 15 were waited for; matrix products, arithmetic and copies ran while one was open for 14% of the time, Pallas kernels for 18%

profile of v4, /device:TPU:20, one launch (start us, length us, event | category | flops | bytes accessed | tf_op | source)
XLA Modules:
  0.0 587.5 jit_solution(13165399584555496317)
XLA Ops:
  27.9 36.6 %collective-permute-done.refs_1_.refs_4_ = bf16[16,32,768]{2,1,0:T(8,128)(2,1)S(1)} collective-permute-done((bf16[16,32,768]{2,1,0:T(8,128)(2,1)}, bf16[16,32,768]{2,1,0:T(8,128)(2,1)S(1)}, u32[]{:S(2)}, u32[]{:S(2)}) %collective-permute-start) | collective-permute-done | bytes 786464 | tf_op jit(solution)/shard_map/ppermute | solution.py:169
  67.7 4.8 collective-permute-start.6
  76.1 7.9 %convolution_convert_fusion.1 = bf16[16,256,768]{2,1,0:T(8,128)(2,1)} fusion(bf16[256,16,256]{2,0,1:T(8,128)(2,1)} %all-gather.3.cloned.1.call-done, bf16[16,256,768]{2,1,0:T(8,128)(2,1)} %bitcast.44), kind=kOutput, calls=%fused_computation.20 | convolution fusion | flops 1613758464 | bytes 14680064 | tf_op jit(solution)/shard_map/ibk,bkd->bid/dot_general | solution.py:198
  84.1 14.2 %collective-permute-done.2.refs_1_.refs_5_ = bf16[16,32,768]{2,1,0:T(8,128)(2,1)S(1)} collective-permute-done((bf16[16,32,768]{2,1,0:T(8,128)(2,1)}, bf16[16,32,768]{2,1,0:T(8,128)(2,1)S(1)}, u32[]{:S(2)}, u32[]{:S(2)}) %collective-permute-start.2) | collective-permute-done | bytes 786464 | tf_op jit(solution)/shard_map/ppermute | solution.py:169
  101.1 4.7 collective-permute-start.9
  110.6 39.6 %collective-permute-done.5.refs_1_.refs_6_ = bf16[16,32,768]{2,1,0:T(8,128)(2,1)} collective-permute-done((bf16[16,32,768]{2,1,0:T(8,128)(2,1)}, bf16[16,32,768]{2,1,0:T(8,128)(2,1)}, u32[]{:S(2)}, u32[]{:S(2)}) %collective-permute-start.5) | collective-permute-done | bytes 786464 | tf_op jit(solution)/shard_map/ppermute | solution.py:169
  150.2 17.7 %collective-permute-done.8.refs_1_.refs_7_ = bf16[16,32,768]{2,1,0:T(8,128)(2,1)S(1)} collective-permute-done((bf16[16,32,768]{2,1,0:T(8,128)(2,1)}, bf16[16,32,768]{2,1,0:T(8,128)(2,1)S(1)}, u32[]{:S(2)}, u32[]{:S(2)}) %collective-permute-start.8) | collective-permute-done | bytes 786464 | tf_op jit(solution)/shard_map/ppermute | solution.py:169
  168.8 7.4 %place.3 = bf16[8,16,32,768]{3,2,1,0:T(8,128)(2,1)} custom-call(s32[1]{0:T(128)} %bitcast.1.at_ref.where_ref, bf16[16,32,768]{2,1,0:T(8,128)(2,1)} %upstream.15.refs_0_, bf16[16,32,768]{2,1,0:T(8,128)(2,1)} %copy-done.5, bf16[16,32,768]{2,1,0:T(8,128)(2,1)} %collective-permute-done.3.refs_1_.refs_2_, ...), custom_call_target="tpu_custom_call" | custom-call | flops 393216 | bytes 12582912 | tf_op jit(solution)/shard_map/place/pallas_call | solution.py:110
  176.2 10.9 %convert_bitcast_fusion.1 = bf16[128,32,768]{2,0,1:T(8,128)(2,1)S(1)} fusion(bf16[128,32,128]{2,0,1:T(8,128)(2,1)} %all-gather.5.cloned.1.call-done, bf16[128,32,768]{2,1,0:T(8,128)(2,1)} %bitcast.96), kind=kOutput, calls=%fused_computation.9 | convolution fusion | flops 808452096 | bytes 13631488 | tf_op jit(solution)/shard_map/ijk,ijd->kjd/dot_general | solution.py:180
  187.1 6.2 %copy.17 = bf16[128,32,768]{2,1,0:T(8,128)(2,1)} copy(bf16[128,32,768]{2,0,1:T(8,128)(2,1)S(1)} %convert_bitcast_fusion.1) | data formatting | bytes 12582912 | tf_op jit(solution)/shard_map/convert_element_type | solution.py:180
  213.6 17.9 %collective-permute-done.11.refs_5_.refs_1_ = bf16[16,32,768]{2,1,0:T(8,128)(2,1)S(1)} collective-permute-done((bf16[16,32,768]{2,1,0:T(8,128)(2,1)}, bf16[16,32,768]{2,1,0:T(8,128)(2,1)S(1)}, u32[]{:S(2)}, u32[]{:S(2)}) %collective-permute-start.11) | collective-permute-done | bytes 786464 | tf_op jit(solution)/shard_map/ppermute | solution.py:169
  234.3 4.6 collective-permute-start.14
  241.5 40.4 %collective-permute-done.12.refs_6_.refs_1_ = bf16[16,32,768]{2,1,0:T(8,128)(2,1)} collective-permute-done((bf16[16,32,768]{2,1,0:T(8,128)(2,1)}, bf16[16,32,768]{2,1,0:T(8,128)(2,1)}, u32[]{:S(2)}, u32[]{:S(2)}) %collective-permute-start.12) | collective-permute-done | bytes 786464 | tf_op jit(solution)/shard_map/ppermute | solution.py:169
  282.0 33.8 %collective-permute-done.13.refs_7_.refs_1_ = bf16[16,32,768]{2,1,0:T(8,128)(2,1)} collective-permute-done((bf16[16,32,768]{2,1,0:T(8,128)(2,1)}, bf16[16,32,768]{2,1,0:T(8,128)(2,1)}, u32[]{:S(2)}, u32[]{:S(2)}) %collective-permute-start.13) | collective-permute-done | bytes 786464 | tf_op jit(solution)/shard_map/ppermute | solution.py:169
  315.7 6.8 %place.4 = bf16[8,16,32,768]{3,2,1,0:T(8,128)(2,1)} custom-call(s32[1]{0:T(128)} %bitcast.1.at_ref.where_ref, bf16[16,32,768]{2,1,0:T(8,128)(2,1)} %pick.24.refs_0_, bf16[16,32,768]{2,1,0:T(8,128)(2,1)} %copy-done.8, bf16[16,32,768]{2,1,0:T(8,128)(2,1)} %collective-permute-done.7.refs_2_.refs_1_, ...), custom_call_target="tpu_custom_call" | custom-call | flops 393216 | bytes 12582912 | tf_op jit(solution)/shard_map/place/pallas_call | solution.py:110
  322.6 10.8 %fusion.6 = f32[32,128,128]{2,1,0:T(8,128)} fusion(bf16[128,32,768]{2,1,0:T(8,128)(2,1)} %bitcast.100, bf16[128,32,768]{2,1,0:T(8,128)(2,1)S(1)} %bitcast.99), kind=kOutput, calls=%fused_computation.10 | convolution fusion | flops 805306368 | bytes 14680064 | tf_op jit(solution)/shard_map/ijd,kjd->ijk/dot_general | solution.py:203
  341.6 3.4 collective-permute-start.17
  347.1 7.8 %convert_bitcast_fusion = bf16[128,32,768]{2,0,1:T(8,128)(2,1)S(1)} fusion(bf16[128,32,128]{2,0,1:T(8,128)(2,1)S(1)} %copy-done.1, bf16[128,32,768]{2,1,0:T(8,128)(2,1)S(1)} %bitcast.103), kind=kOutput, calls=%fused_computation.8 | convolution fusion | flops 808452096 | bytes 13631488 | tf_op jit(solution)/shard_map/ijk,kjd->ijd/dot_general | solution.py:186
  354.9 6.2 %copy.19 = bf16[128,32,768]{2,1,0:T(8,128)(2,1)} copy(bf16[128,32,768]{2,0,1:T(8,128)(2,1)S(1)} %convert_bitcast_fusion) | data formatting | bytes 12582912 | tf_op jit(solution)/shard_map/convert_element_type | solution.py:186
  371.1 9.6 %fusion.5.slope_ref = bf16[16,8,32,768]{3,2,1,0:T(8,128)(2,1)} fusion(bf16[16,8,32,768]{3,2,1,0:T(8,128)(2,1)S(1)} %bitcast.48, bf16[16,8,32,768]{3,2,1,0:T(8,128)(2,1)} %bitcast.84), kind=kLoop, calls=%fused_computation.7 | loop fusion | flops 34603008 | bytes 18874368 | tf_op jit(solution)/shard_map/convert_element_type | solution.py:213
  388.1 8.7 %collective-permute-done.17.refs_1_.refs_2_ = bf16[16,32,768]{2,1,0:T(8,128)(2,1)} collective-permute-done((bf16[16,32,768]{2,1,0:T(8,128)(2,1)}, bf16[16,32,768]{2,1,0:T(8,128)(2,1)}, u32[]{:S(2)}, u32[]{:S(2)}) %collective-permute-start.17) | collective-permute-done | bytes 786464 | tf_op jit(solution)/shard_map/ppermute | solution.py:169
  399.2 13.6 %collective-permute-done.18.refs_1_.refs_6_ = bf16[16,32,768]{2,1,0:T(8,128)(2,1)} collective-permute-done((bf16[16,32,768]{2,1,0:T(8,128)(2,1)S(1)}, bf16[16,32,768]{2,1,0:T(8,128)(2,1)}, u32[]{:S(2)}, u32[]{:S(2)}) %collective-permute-start.18) | collective-permute-done | bytes 786464 | tf_op jit(solution)/shard_map/ppermute | solution.py:169
  414.8 13.7 %collective-permute-done.19.refs_1_.refs_3_ = bf16[16,32,768]{2,1,0:T(8,128)(2,1)S(1)} collective-permute-done((bf16[16,32,768]{2,1,0:T(8,128)(2,1)}, bf16[16,32,768]{2,1,0:T(8,128)(2,1)S(1)}, u32[]{:S(2)}, u32[]{:S(2)}) %collective-permute-start.19) | collective-permute-done | bytes 786464 | tf_op jit(solution)/shard_map/ppermute | solution.py:169
  432.4 46.5 %collective-permute-done.20.refs_1_.refs_7_ = bf16[16,32,768]{2,1,0:T(8,128)(2,1)} collective-permute-done((bf16[16,32,768]{2,1,0:T(8,128)(2,1)}, bf16[16,32,768]{2,1,0:T(8,128)(2,1)}, u32[]{:S(2)}, u32[]{:S(2)}) %collective-permute-start.20) | collective-permute-done | bytes 786464 | tf_op jit(solution)/shard_map/ppermute | solution.py:169
  482.4 6.8 %place.5 = bf16[16,8,32,768]{3,2,1,0:T(8,128)(2,1)} custom-call(s32[1]{0:T(128)} %bitcast.1.at_ref.where_ref, bf16[16,32,768]{2,1,0:T(8,128)(2,1)} %pick.44.refs_0_, bf16[16,32,768]{2,1,0:T(8,128)(2,1)} %collective-permute-done.15.refs_1_, bf16[16,32,768]{2,1,0:T(8,128)(2,1)} %collective-permute-done.17.refs_1_.refs_2_, bf16[16,32,768]{2,1,0:T(8,128)(2,1)} %copy-done.11, ...), custom_call_target="tpu_custom_call" | custom-call | flops 393216 | bytes 12582912 | tf_op jit(solution)/shard_map/place/pallas_call | solution.py:110
  489.3 4.6 fusion.18
  493.9 4.7 fusion.13.refs_3_
  498.6 7.5 %convolution_convert_fusion = bf16[16,768,256]{1,2,0:T(8,128)(2,1)} fusion(bf16[16,256,768]{2,1,0:T(8,128)(2,1)} %bitcast.86, bf16[256,16,256]{2,0,1:T(8,128)(2,1)S(1)} %copy-done), kind=kOutput, calls=%fused_computation.19 | convolution fusion | flops 1613758464 | bytes 14680064 | tf_op jit(solution)/shard_map/ibk,bid->bkd/dot_general | solution.py:193
  506.0 3.6 collective-permute-done.21.refs_1_.y_ref
  511.5 2.8 collective-permute-start.24
  531.3 29.3 %collective-permute-done.25.y_ref = bf16[16,32,768]{2,1,0:T(8,128)(2,1)} collective-permute-done((bf16[16,32,768]{2,1,0:T(8,128)(2,1)}, bf16[16,32,768]{2,1,0:T(8,128)(2,1)}, u32[]{:S(2)}, u32[]{:S(2)}) %collective-permute-start.25) | collective-permute-done | bytes 786464 | tf_op jit(solution)/shard_map/ppermute | solution.py:169
  565.5 12.7 %collective-permute-done.23.y_ref = bf16[16,32,768]{2,1,0:T(8,128)(2,1)} collective-permute-done((bf16[16,32,768]{2,1,0:T(8,128)(2,1)}, bf16[16,32,768]{2,1,0:T(8,128)(2,1)}, u32[]{:S(2)}, u32[]{:S(2)}) %collective-permute-start.23) | collective-permute-done | bytes 786464 | tf_op jit(solution)/shard_map/ppermute | solution.py:169
  (136 shorter events, 127.3 us)
Async XLA Ops:
  7.2 69.0 %all-gather.3.cloned.1.call-start = ((), (), s32[]{:S(2)}) async-start(), calls=%async_computation.2 | async-start | bytes 2621440 | tf_op jit(solution)/shard_map/all_gather | solution.py:174
  9.2 167.0 %all-gather.5.cloned.1.call-start = ((), (), s32[]{:S(2)}) async-start(), calls=%async_computation.3 | async-start | bytes 1310720 | tf_op jit(solution)/shard_map/all_gather | solution.py:175
  11.6 52.9 %collective-permute-start = (bf16[16,32,768]{2,1,0:T(8,128)(2,1)}, bf16[16,32,768]{2,1,0:T(8,128)(2,1)S(1)}, u32[]{:S(2)}, u32[]{:S(2)}) collective-permute-start(bf16[16,32,768]{2,1,0:T(8,128)(2,1)} %upstream.8.refs_0_), channel_id=1, source_target_pairs={{0,4},{1,5},{2,6},{3,7},{4,0},{5,1},{6,2},{7,3},{8,12},{9,13},{10,... | collective-permute-start | bytes 2359304 | tf_op jit(solution)/shard_map/ppermute | solution.py:169
  14.3 58.2 %collective-permute-start.1 = (bf16[16,32,768]{2,1,0:T(8,128)(2,1)}, bf16[16,32,768]{2,1,0:T(8,128)(2,1)S(1)}, u32[]{:S(2)}, u32[]{:S(2)}) collective-permute-start(bf16[16,32,768]{2,1,0:T(8,128)(2,1)} %upstream.9.refs_0_), channel_id=1, source_target_pairs={{0,1},{1,0},{2,3},{3,2},{4,5},{5,4},{6,7},{7,6},{8,9},{9,8},{10,11... | collective-permute-start | bytes 2359304 | tf_op jit(solution)/shard_map/ppermute | solution.py:169
  16.6 546.4 %reduce-scatter.5.cloned.1.call-start = ((), (), s32[]{:S(2)}) async-start(), calls=%async_computation.5 | async-start | bytes 2621440 | tf_op jit(solution)/shard_map/reduce_scatter | solution.py:202
  19.1 79.1 %collective-permute-start.2 = (bf16[16,32,768]{2,1,0:T(8,128)(2,1)}, bf16[16,32,768]{2,1,0:T(8,128)(2,1)S(1)}, u32[]{:S(2)}, u32[]{:S(2)}) collective-permute-start(bf16[16,32,768]{2,1,0:T(8,128)(2,1)} %upstream.10.refs_0_), channel_id=1, source_target_pairs={{0,5},{1,4},{2,7},{3,6},{4,1},{5,0},{6,3},{7,2},{8,13},{9,12},{10,... | collective-permute-start | bytes 2359304 | tf_op jit(solution)/shard_map/ppermute | solution.py:169
  24.0 81.8 %collective-permute-start.3 = (bf16[16,32,768]{2,1,0:T(8,128)(2,1)}, bf16[16,32,768]{2,1,0:T(8,128)(2,1)}, u32[]{:S(2)}, u32[]{:S(2)}) collective-permute-start(bf16[16,32,768]{2,1,0:T(8,128)(2,1)} %upstream.11.refs_0_), channel_id=1, source_target_pairs={{0,2},{1,3},{2,0},{3,1},{4,6},{5,7},{6,4},{7,5},{8,10},{9,11},{10,... | collective-permute-start | bytes 2359304 | tf_op jit(solution)/shard_map/ppermute | solution.py:169
  27.9 122.3 %collective-permute-start.5 = (bf16[16,32,768]{2,1,0:T(8,128)(2,1)}, bf16[16,32,768]{2,1,0:T(8,128)(2,1)}, u32[]{:S(2)}, u32[]{:S(2)}) collective-permute-start(bf16[16,32,768]{2,1,0:T(8,128)(2,1)} %upstream.12.refs_0_), channel_id=1, source_target_pairs={{0,6},{1,7},{2,4},{3,5},{4,2},{5,3},{6,0},{7,1},{8,14},{9,15},{10,... | collective-permute-start | bytes 2359304 | tf_op jit(solution)/shard_map/ppermute | solution.py:169
  67.7 100.2 %collective-permute-start.6 = (bf16[16,32,768]{2,1,0:T(8,128)(2,1)}, bf16[16,32,768]{2,1,0:T(8,128)(2,1)}, u32[]{:S(2)}, u32[]{:S(2)}) collective-permute-start(bf16[16,32,768]{2,1,0:T(8,128)(2,1)} %upstream.13.refs_0_), channel_id=1, source_target_pairs={{0,3},{1,2},{2,1},{3,0},{4,7},{5,6},{6,5},{7,4},{8,11},{9,10},{10,... | collective-permute-start | bytes 2359304 | tf_op jit(solution)/shard_map/ppermute | solution.py:169
  75.7 92.2 %collective-permute-start.8 = (bf16[16,32,768]{2,1,0:T(8,128)(2,1)}, bf16[16,32,768]{2,1,0:T(8,128)(2,1)S(1)}, u32[]{:S(2)}, u32[]{:S(2)}) collective-permute-start(bf16[16,32,768]{2,1,0:T(8,128)(2,1)} %upstream.14.refs_0_), channel_id=1, source_target_pairs={{0,7},{1,6},{2,5},{3,4},{4,3},{5,2},{6,1},{7,0},{8,15},{9,14},{10,... | collective-permute-start | bytes 2359304 | tf_op jit(solution)/shard_map/ppermute | solution.py:169
  101.1 101.5 %collective-permute-start.9 = (bf16[16,32,768]{2,1,0:T(8,128)(2,1)}, bf16[16,32,768]{2,1,0:T(8,128)(2,1)S(1)}, u32[]{:S(2)}, u32[]{:S(2)}) collective-permute-start(bf16[16,32,768]{2,1,0:T(8,128)(2,1)} %pick.25.refs_0_), channel_id=1, source_target_pairs={{0,4},{1,5},{2,6},{3,7},{4,0},{5,1},{6,2},{7,3},{8,12},{9,13},{10,... | collective-permute-start | bytes 2359304 | tf_op jit(solution)/shard_map/ppermute | solution.py:169
  107.7 97.6 %collective-permute-start.4 = (bf16[16,32,768]{2,1,0:T(8,128)(2,1)}, bf16[16,32,768]{2,1,0:T(8,128)(2,1)S(1)}, u32[]{:S(2)}, u32[]{:S(2)}) collective-permute-start(bf16[16,32,768]{2,1,0:T(8,128)(2,1)} %pick.26.refs_0_), channel_id=1, source_target_pairs={{0,1},{1,0},{2,3},{3,2},{4,5},{5,4},{6,7},{7,6},{8,9},{9,8},{10,11... | collective-permute-start | bytes 2359304 | tf_op jit(solution)/shard_map/ppermute | solution.py:169
  195.3 36.1 %collective-permute-start.11 = (bf16[16,32,768]{2,1,0:T(8,128)(2,1)}, bf16[16,32,768]{2,1,0:T(8,128)(2,1)S(1)}, u32[]{:S(2)}, u32[]{:S(2)}) collective-permute-start(bf16[16,32,768]{2,1,0:T(8,128)(2,1)} %pick.27.refs_0_), channel_id=1, source_target_pairs={{0,5},{1,4},{2,7},{3,6},{4,1},{5,0},{6,3},{7,2},{8,13},{9,12},{10,... | collective-permute-start | bytes 2359304 | tf_op jit(solution)/shard_map/ppermute | solution.py:169
  197.2 41.7 %collective-permute-start.7 = (bf16[16,32,768]{2,1,0:T(8,128)(2,1)}, bf16[16,32,768]{2,1,0:T(8,128)(2,1)}, u32[]{:S(2)}, u32[]{:S(2)}) collective-permute-start(bf16[16,32,768]{2,1,0:T(8,128)(2,1)} %pick.28.refs_0_), channel_id=1, source_target_pairs={{0,2},{1,3},{2,0},{3,1},{4,6},{5,7},{6,4},{7,5},{8,10},{9,11},{10,... | collective-permute-start | bytes 2359304 | tf_op jit(solution)/shard_map/ppermute | solution.py:169
  201.0 81.0 %collective-permute-start.12 = (bf16[16,32,768]{2,1,0:T(8,128)(2,1)}, bf16[16,32,768]{2,1,0:T(8,128)(2,1)}, u32[]{:S(2)}, u32[]{:S(2)}) collective-permute-start(bf16[16,32,768]{2,1,0:T(8,128)(2,1)} %pick.29.refs_0_), channel_id=1, source_target_pairs={{0,6},{1,7},{2,4},{3,5},{4,2},{5,3},{6,0},{7,1},{8,14},{9,15},{10,... | collective-permute-start | bytes 2359304 | tf_op jit(solution)/shard_map/ppermute | solution.py:169
  208.2 107.6 %collective-permute-start.13 = (bf16[16,32,768]{2,1,0:T(8,128)(2,1)}, bf16[16,32,768]{2,1,0:T(8,128)(2,1)}, u32[]{:S(2)}, u32[]{:S(2)}) collective-permute-start(bf16[16,32,768]{2,1,0:T(8,128)(2,1)} %pick.31.refs_0_), channel_id=1, source_target_pairs={{0,7},{1,6},{2,5},{3,4},{4,3},{5,2},{6,1},{7,0},{8,15},{9,14},{10,... | collective-permute-start | bytes 2359304 | tf_op jit(solution)/shard_map/ppermute | solution.py:169
  209.6 106.1 %collective-permute-start.10 = (bf16[16,32,768]{2,1,0:T(8,128)(2,1)S(1)}, bf16[16,32,768]{2,1,0:T(8,128)(2,1)}, u32[]{:S(2)}, u32[]{:S(2)}) collective-permute-start(bf16[16,32,768]{2,1,0:T(8,128)(2,1)S(1)} %copy-done.7), channel_id=1, source_target_pairs={{0,3},{1,2},{2,1},{3,0},{4,7},{5,6},{6,5},{7,4},{8,11},{9,10},{10,... | collective-permute-start | bytes 2359304 | tf_op jit(solution)/shard_map/ppermute | solution.py:169
  234.3 127.8 %collective-permute-start.14 = (bf16[16,32,768]{2,1,0:T(8,128)(2,1)}, bf16[16,32,768]{2,1,0:T(8,128)(2,1)S(1)}, u32[]{:S(2)}, u32[]{:S(2)}) collective-permute-start(bf16[16,32,768]{2,1,0:T(8,128)(2,1)} %pick.32.refs_0_), channel_id=1, source_target_pairs={{0,4},{1,5},{2,6},{3,7},{4,0},{5,1},{6,2},{7,3},{8,12},{9,13},{10,... | collective-permute-start | bytes 2359304 | tf_op jit(solution)/shard_map/ppermute | solution.py:169
  241.0 126.5 %collective-permute-start.15 = (bf16[16,32,768]{2,1,0:T(8,128)(2,1)}, bf16[16,32,768]{2,1,0:T(8,128)(2,1)}, u32[]{:S(2)}, u32[]{:S(2)}) collective-permute-start(bf16[16,32,768]{2,1,0:T(8,128)(2,1)} %pick.33.refs_0_), channel_id=1, source_target_pairs={{0,1},{1,0},{2,3},{3,2},{4,5},{5,4},{6,7},{7,6},{8,9},{9,8},{10,11... | collective-permute-start | bytes 2359304 | tf_op jit(solution)/shard_map/ppermute | solution.py:169
  337.4 225.6 %reduce-scatter.3.cloned.1.call-start = ((), (), s32[]{:S(2)}) async-start(), calls=%async_computation.4 | async-start | bytes 5242880 | tf_op jit(solution)/shard_map/reduce_scatter | solution.py:209
  339.6 44.9 %collective-permute-start.16 = (bf16[16,32,768]{2,1,0:T(8,128)(2,1)}, bf16[16,32,768]{2,1,0:T(8,128)(2,1)}, u32[]{:S(2)}, u32[]{:S(2)}) collective-permute-start(bf16[16,32,768]{2,1,0:T(8,128)(2,1)} %pick.34.refs_0_), channel_id=1, source_target_pairs={{0,5},{1,4},{2,7},{3,6},{4,1},{5,0},{6,3},{7,2},{8,13},{9,12},{10,... | collective-permute-start | bytes 2359304 | tf_op jit(solution)/shard_map/ppermute | solution.py:169
  341.6 55.2 %collective-permute-start.17 = (bf16[16,32,768]{2,1,0:T(8,128)(2,1)}, bf16[16,32,768]{2,1,0:T(8,128)(2,1)}, u32[]{:S(2)}, u32[]{:S(2)}) collective-permute-start(bf16[16,32,768]{2,1,0:T(8,128)(2,1)} %pick.35.refs_0_), channel_id=1, source_target_pairs={{0,2},{1,3},{2,0},{3,1},{4,6},{5,7},{6,4},{7,5},{8,10},{9,11},{10,... | collective-permute-start | bytes 2359304 | tf_op jit(solution)/shard_map/ppermute | solution.py:169
  361.1 51.8 %collective-permute-start.18 = (bf16[16,32,768]{2,1,0:T(8,128)(2,1)S(1)}, bf16[16,32,768]{2,1,0:T(8,128)(2,1)}, u32[]{:S(2)}, u32[]{:S(2)}) collective-permute-start(bf16[16,32,768]{2,1,0:T(8,128)(2,1)S(1)} %copy-done.6), channel_id=1, source_target_pairs={{0,6},{1,7},{2,4},{3,5},{4,2},{5,3},{6,0},{7,1},{8,14},{9,15},{10,... | collective-permute-start | bytes 2359304 | tf_op jit(solution)/shard_map/ppermute | solution.py:169
  365.5 63.0 %collective-permute-start.19 = (bf16[16,32,768]{2,1,0:T(8,128)(2,1)}, bf16[16,32,768]{2,1,0:T(8,128)(2,1)S(1)}, u32[]{:S(2)}, u32[]{:S(2)}) collective-permute-start(bf16[16,32,768]{2,1,0:T(8,128)(2,1)} %pick.37.refs_0_), channel_id=1, source_target_pairs={{0,3},{1,2},{2,1},{3,0},{4,7},{5,6},{6,5},{7,4},{8,11},{9,10},{10,... | collective-permute-start | bytes 2359304 | tf_op jit(solution)/shard_map/ppermute | solution.py:169
  369.4 109.5 %collective-permute-start.20 = (bf16[16,32,768]{2,1,0:T(8,128)(2,1)}, bf16[16,32,768]{2,1,0:T(8,128)(2,1)}, u32[]{:S(2)}, u32[]{:S(2)}) collective-permute-start(bf16[16,32,768]{2,1,0:T(8,128)(2,1)} %pick.38.refs_0_), channel_id=1, source_target_pairs={{0,7},{1,6},{2,5},{3,4},{4,3},{5,2},{6,1},{7,0},{8,15},{9,14},{10,... | collective-permute-start | bytes 2359304 | tf_op jit(solution)/shard_map/ppermute | solution.py:169
  386.4 123.2 %collective-permute-start.21 = (bf16[16,32,768]{2,1,0:T(8,128)(2,1)}, bf16[16,32,768]{2,1,0:T(8,128)(2,1)}, u32[]{:S(2)}, u32[]{:S(2)}) collective-permute-start(bf16[16,32,768]{2,1,0:T(8,128)(2,1)} %pick.39.refs_0_), channel_id=1, source_target_pairs={{0,4},{1,5},{2,6},{3,7},{4,0},{5,1},{6,2},{7,3},{8,12},{9,13},{10,... | collective-permute-start | bytes 2359304 | tf_op jit(solution)/shard_map/ppermute | solution.py:169
  398.7 120.8 %collective-permute-start.22 = (bf16[16,32,768]{2,1,0:T(8,128)(2,1)}, bf16[16,32,768]{2,1,0:T(8,128)(2,1)}, u32[]{:S(2)}, u32[]{:S(2)}) collective-permute-start(bf16[16,32,768]{2,1,0:T(8,128)(2,1)} %pick.40.refs_0_), channel_id=1, source_target_pairs={{0,1},{1,0},{2,3},{3,2},{4,5},{5,4},{6,7},{7,6},{8,9},{9,8},{10,11... | collective-permute-start | bytes 2359304 | tf_op jit(solution)/shard_map/ppermute | solution.py:169
  414.8 111.7 %collective-permute-start.27 = (bf16[16,32,768]{2,1,0:T(8,128)(2,1)}, bf16[16,32,768]{2,1,0:T(8,128)(2,1)}, u32[]{:S(2)}, u32[]{:S(2)}) collective-permute-start(bf16[16,32,768]{2,1,0:T(8,128)(2,1)} %pick.41.refs_0_), channel_id=1, source_target_pairs={{0,5},{1,4},{2,7},{3,6},{4,1},{5,0},{6,3},{7,2},{8,13},{9,12},{10,... | collective-permute-start | bytes 2359304 | tf_op jit(solution)/shard_map/ppermute | solution.py:169
  431.3 97.6 %collective-permute-start.26 = (bf16[16,32,768]{2,1,0:T(8,128)(2,1)}, bf16[16,32,768]{2,1,0:T(8,128)(2,1)}, u32[]{:S(2)}, u32[]{:S(2)}) collective-permute-start(bf16[16,32,768]{2,1,0:T(8,128)(2,1)} %pick.42.refs_0_), channel_id=1, source_target_pairs={{0,2},{1,3},{2,0},{3,1},{4,6},{5,7},{6,4},{7,5},{8,10},{9,11},{10,... | collective-permute-start | bytes 2359304 | tf_op jit(solution)/shard_map/ppermute | solution.py:169
  480.8 79.8 %collective-permute-start.25 = (bf16[16,32,768]{2,1,0:T(8,128)(2,1)}, bf16[16,32,768]{2,1,0:T(8,128)(2,1)}, u32[]{:S(2)}, u32[]{:S(2)}) collective-permute-start(bf16[16,32,768]{2,1,0:T(8,128)(2,1)} %pick.43.refs_0_), channel_id=1, source_target_pairs={{0,6},{1,7},{2,4},{3,5},{4,2},{5,3},{6,0},{7,1},{8,14},{9,15},{10,... | collective-permute-start | bytes 2359304 | tf_op jit(solution)/shard_map/ppermute | solution.py:169
  511.5 51.5 %collective-permute-start.24 = (bf16[16,32,768]{2,1,0:T(8,128)(2,1)}, bf16[16,32,768]{2,1,0:T(8,128)(2,1)}, u32[]{:S(2)}, u32[]{:S(2)}) collective-permute-start(bf16[16,32,768]{2,1,0:T(8,128)(2,1)} %pick.45.refs_0_), channel_id=1, source_target_pairs={{0,3},{1,2},{2,1},{3,0},{4,7},{5,6},{6,5},{7,4},{8,11},{9,10},{10,... | collective-permute-start | bytes 2359304 | tf_op jit(solution)/shard_map/ppermute | solution.py:169
  521.4 56.7 %collective-permute-start.23 = (bf16[16,32,768]{2,1,0:T(8,128)(2,1)}, bf16[16,32,768]{2,1,0:T(8,128)(2,1)}, u32[]{:S(2)}, u32[]{:S(2)}) collective-permute-start(bf16[16,32,768]{2,1,0:T(8,128)(2,1)} %pick.46), channel_id=1, source_target_pairs={{0,7},{1,6},{2,5},{3,4},{4,3},{5,2},{6,1},{7,0},{8,15},{9,14},{10,... | collective-permute-start | bytes 2359304 | tf_op jit(solution)/shard_map/ppermute | solution.py:169
  (20 other events, 227.6 us)
Sparse Core Ops, SparseCore 0:
  10.1 22.6 all-gather.2
  34.4 16.7 all-gather.4
  337.5 30.5 reduce-scatter.4
  498.7 43.8 reduce-scatter.2

commit v5 on v4

--- a/solution.py
+++ b/solution.py
@@ -9,7 +9,7 @@
 
 ROOM = pltpu.CompilerParams(vmem_limit_bytes=56 * 1024 * 1024)
 STEPS = 2
-WINDOW = 5
+WINDOW = 6
 ANYWHERE = pl.BlockSpec(memory_space=pl.ANY)
 
 
@@ -175,6 +175,14 @@
     second = lax.all_gather(second_factor, "dp", axis=0, tiled=True)
     made = {}
 
+    def to_slope(cut):
+        x_wide = x.astype(jnp.float32)
+        c_wide = cotangent.reshape(x.shape).astype(jnp.float32)
+        logistic = jax.nn.sigmoid(x_wide)
+        slope = (c_wide * logistic * (1.0 + x_wide * (1.0 - logistic))).astype(bf16)
+        made["slope"] = slope
+        return [slope]
+
     def to_back(cut):
         made["up"] = place(up_pieces, where[0], 0, []).reshape(column_shape)
         back = jnp.einsum("ijk,ijd->kjd", second, made["up"], **wide).astype(bf16)
@@ -194,7 +202,7 @@
         made["folded"] = folded.reshape(rows)
         return [made["folded"], made["first"]]
 
-    up_pieces = exchange(upstream_kernel, [x_rows, c_rows], 1, "upstream", distances)
+    up_pieces = exchange(upstream_kernel, [x_rows, c_rows], 1, "upstream", distances, to_slope)
     mixed = jnp.einsum("ibk,bkd->bid", first, x, **wide).astype(bf16).reshape(rows)
     mixed_pieces = exchange(pick_kernel, [mixed], 1, "pick", distances, to_back)
     grad_pieces = exchange(pick_kernel, [made["back"]], 0, "pick", distances, to_product)
@@ -207,11 +215,7 @@
     )
     output = exchange(pick_kernel, [made["product"]], 0, "pick", distances, to_folded)
     first_grad = lax.psum_scatter(made["first"], "dp", scatter_dimension=0, tiled=True)
-    x_wide = x.astype(jnp.float32)
-    c_wide = cotangent.reshape(x.shape).astype(jnp.float32)
-    logistic = jax.nn.sigmoid(x_wide)
-    slope = (c_wide * logistic * (1.0 + x_wide * (1.0 - logistic))).astype(bf16)
-    slope, grad_input = slope.reshape(rows), None
+    slope, grad_input = made["slope"].reshape(rows), None
     for d in [0] + distances:
         after = [first_grad, second_grad] if d == distances[-2] else []
         grad_input = final_piece(output[d], slope, made["folded"], grad_input, where[d], after)

time: 593 us -> 595 us (level)
  other arithmetic: 15.8 us -> 26.5 us
  local copies, waits for them, and re-layouts: 25.5 us -> 19.4 us
    convert_element_type x1 -> x2, other arithmetic: 9.58 us -> 20.3 us  [to_slope(): slope = (c_wide * logistic * (1.0 + x_wide * (1.0 - logistic))).astype(bf16)]
    unnamed x42 -> x38, local copies, waits for them, and re-layouts: 10.8 us -> 4.67 us
  transfers between devices with their start and end apart: 32 -> 32, of which waited for: 15 -> 15; matrix products, arithmetic and copies ran while one was open for 14% -> 16% of each run, Pallas kernels for 18% -> 18%
where the time goes in v5:
time: 595 us; the launch traced here: 588 us
  waiting for transfers between devices  326 us (55%)
  Pallas kernels  106 us (18%)
  matrix products  49.6 us (8%)
  starting transfers between devices  45.7 us (8%)
  other arithmetic  26.5 us (4%)
  local copies, waits for them, and re-layouts  19.4 us (3%)
  between operations  14.4 us (2%)
    ppermute x28, waiting for transfers between devices, exchange(): got[d] = lax.ppermute(cuts[-1], 'seq', [(n, n ^ d) for n in range(owners)])  326 us
    pallas_call x32, Pallas kernels, piece_call(): pl.pallas_call(kernel, grid_spec=pltpu.PrefetchScalarGridSpec(num_scalar_...  65.8 us
    ppermute x28, starting transfers between devices, exchange(): got[d] = lax.ppermute(cuts[-1], 'seq', [(n, n ^ d) for n in range(owners)])  45.6 us
    pallas_call x3, Pallas kernels, place(): pl.pallas_call(functools.partial(place_kernel, owners), grid_spec=pltpu.P...  21.1 us
    convert_element_type x2, other arithmetic, to_slope(): slope = (c_wide * logistic * (1.0 + x_wide * (1.0 - logistic))).astype(bf16)  20.3 us
    pallas_call x8, Pallas kernels, final_piece(): pl.pallas_call(final_kernel, grid_spec=pltpu.PrefetchScalarGridSpec(num_s...  19.4 us
  transfers between devices with their start and end apart: 32, of which 15 were waited for; matrix products, arithmetic and copies ran while one was open for 16% of the time, Pallas kernels for 18%

profile of v5, /device:TPU:20, one launch (start us, length us, event | category | flops | bytes accessed | tf_op | source)
XLA Modules:
  0.0 587.6 jit_solution(11581436614893269129)
XLA Ops:
  31.2 10.7 %fusion.5.refs_2_ = bf16[16,256,768]{2,1,0:T(8,128)(2,1)} fusion(bf16[16,256,768]{2,1,0:T(8,128)(2,1)} %bitcast.45, bf16[16,256,768]{2,1,0:T(8,128)(2,1)} %bitcast.59), kind=kLoop, calls=%fused_computation.9 | loop fusion | flops 34603008 | bytes 18874368 | tf_op jit(solution)/shard_map/convert_element_type | solution.py:182
  41.9 38.9 %collective-permute-done.refs_1_.refs_4_ = bf16[16,32,768]{2,1,0:T(8,128)(2,1)S(1)} collective-permute-done((bf16[16,32,768]{2,1,0:T(8,128)(2,1)}, bf16[16,32,768]{2,1,0:T(8,128)(2,1)S(1)}, u32[]{:S(2)}, u32[]{:S(2)}) %collective-permute-start) | collective-permute-done | bytes 786464 | tf_op jit(solution)/shard_map/ppermute | solution.py:169
  80.8 3.3 collective-permute-start.4
  87.9 7.9 %convolution_convert_fusion.1 = bf16[16,256,768]{2,1,0:T(8,128)(2,1)} fusion(bf16[256,16,256]{2,0,1:T(8,128)(2,1)} %all-gather.3.cloned.1.call-done, bf16[16,256,768]{2,1,0:T(8,128)(2,1)} %bitcast.47), kind=kOutput, calls=%fused_computation.29 | convolution fusion | flops 1613758464 | bytes 14680064 | tf_op jit(solution)/shard_map/ibk,bkd->bid/dot_general | solution.py:206
  97.8 4.2 collective-permute-start.10
  106.8 43.4 %collective-permute-done.5.refs_1_.refs_6_ = bf16[16,32,768]{2,1,0:T(8,128)(2,1)} collective-permute-done((bf16[16,32,768]{2,1,0:T(8,128)(2,1)}, bf16[16,32,768]{2,1,0:T(8,128)(2,1)}, u32[]{:S(2)}, u32[]{:S(2)}) %collective-permute-start.5) | collective-permute-done | bytes 786464 | tf_op jit(solution)/shard_map/ppermute | solution.py:169
  150.2 17.8 %collective-permute-done.8.refs_1_.refs_7_ = bf16[16,32,768]{2,1,0:T(8,128)(2,1)} collective-permute-done((bf16[16,32,768]{2,1,0:T(8,128)(2,1)}, bf16[16,32,768]{2,1,0:T(8,128)(2,1)}, u32[]{:S(2)}, u32[]{:S(2)}) %collective-permute-start.8) | collective-permute-done | bytes 786464 | tf_op jit(solution)/shard_map/ppermute | solution.py:169
  168.0 7.4 %place.3 = bf16[8,16,32,768]{3,2,1,0:T(8,128)(2,1)} custom-call(s32[1]{0:T(128)} %bitcast.1.at_ref.where_ref, bf16[16,32,768]{2,1,0:T(8,128)(2,1)} %upstream.15.refs_0_, bf16[16,32,768]{2,1,0:T(8,128)(2,1)} %copy-done.7, bf16[16,32,768]{2,1,0:T(8,128)(2,1)} %collective-permute-done.4.refs_1_.refs_2_, ...), custom_call_target="tpu_custom_call" | custom-call | flops 393216 | bytes 12582912 | tf_op jit(solution)/shard_map/place/pallas_call | solution.py:110
  175.4 10.9 %convert_bitcast_fusion.1 = bf16[128,32,768]{2,0,1:T(8,128)(2,1)S(1)} fusion(bf16[128,32,128]{2,0,1:T(8,128)(2,1)} %all-gather.5.cloned.1.call-done, bf16[128,32,768]{2,1,0:T(8,128)(2,1)} %bitcast.100), kind=kOutput, calls=%fused_computation.18 | convolution fusion | flops 808452096 | bytes 13631488 | tf_op jit(solution)/shard_map/ijk,ijd->kjd/dot_general | solution.py:188
  186.3 6.2 %copy.17 = bf16[128,32,768]{2,1,0:T(8,128)(2,1)} copy(bf16[128,32,768]{2,0,1:T(8,128)(2,1)S(1)} %convert_bitcast_fusion.1) | data formatting | bytes 12582912 | tf_op jit(solution)/shard_map/convert_element_type | solution.py:188
  212.2 18.5 %collective-permute-done.11.refs_5_.refs_1_ = bf16[16,32,768]{2,1,0:T(8,128)(2,1)S(1)} collective-permute-done((bf16[16,32,768]{2,1,0:T(8,128)(2,1)}, bf16[16,32,768]{2,1,0:T(8,128)(2,1)S(1)}, u32[]{:S(2)}, u32[]{:S(2)}) %collective-permute-start.11) | collective-permute-done | bytes 786464 | tf_op jit(solution)/shard_map/ppermute | solution.py:169
  231.6 4.6 collective-permute-start.14
  238.3 26.1 %collective-permute-done.12.refs_6_.refs_1_ = bf16[16,32,768]{2,1,0:T(8,128)(2,1)} collective-permute-done((bf16[16,32,768]{2,1,0:T(8,128)(2,1)}, bf16[16,32,768]{2,1,0:T(8,128)(2,1)}, u32[]{:S(2)}, u32[]{:S(2)}) %collective-permute-start.12) | collective-permute-done | bytes 786464 | tf_op jit(solution)/shard_map/ppermute | solution.py:169
  267.4 47.5 %collective-permute-done.13.refs_7_.refs_1_ = bf16[16,32,768]{2,1,0:T(8,128)(2,1)S(1)} collective-permute-done((bf16[16,32,768]{2,1,0:T(8,128)(2,1)}, bf16[16,32,768]{2,1,0:T(8,128)(2,1)S(1)}, u32[]{:S(2)}, u32[]{:S(2)}) %collective-permute-start.13) | collective-permute-done | bytes 786464 | tf_op jit(solution)/shard_map/ppermute | solution.py:169
  315.8 6.8 %place.4 = bf16[8,16,32,768]{3,2,1,0:T(8,128)(2,1)} custom-call(s32[1]{0:T(128)} %bitcast.1.at_ref.where_ref, bf16[16,32,768]{2,1,0:T(8,128)(2,1)} %pick.24.refs_0_, bf16[16,32,768]{2,1,0:T(8,128)(2,1)} %copy-done.6, bf16[16,32,768]{2,1,0:T(8,128)(2,1)} %collective-permute-done.6.refs_2_.refs_1_, ...), custom_call_target="tpu_custom_call" | custom-call | flops 393216 | bytes 12582912 | tf_op jit(solution)/shard_map/place/pallas_call | solution.py:110
  322.6 10.9 %fusion.12 = f32[32,128,128]{2,1,0:T(8,128)} fusion(bf16[128,32,768]{2,1,0:T(8,128)(2,1)} %bitcast.104, bf16[128,32,768]{2,1,0:T(8,128)(2,1)S(1)} %bitcast.103), kind=kOutput, calls=%fused_computation.19 | convolution fusion | flops 805306368 | bytes 14680064 | tf_op jit(solution)/shard_map/ijd,kjd->ijk/dot_general | solution.py:211
  341.6 3.3 collective-permute-start.17
  350.2 7.8 %convert_bitcast_fusion = bf16[128,32,768]{2,0,1:T(8,128)(2,1)S(1)} fusion(bf16[128,32,128]{2,0,1:T(8,128)(2,1)S(1)} %copy-done.1, bf16[128,32,768]{2,1,0:T(8,128)(2,1)S(1)} %bitcast.107), kind=kOutput, calls=%fused_computation.17 | convolution fusion | flops 808452096 | bytes 13631488 | tf_op jit(solution)/shard_map/ijk,kjd->ijd/dot_general | solution.py:194
  358.0 6.1 %copy.19 = bf16[128,32,768]{2,1,0:T(8,128)(2,1)} copy(bf16[128,32,768]{2,0,1:T(8,128)(2,1)S(1)} %convert_bitcast_fusion) | data formatting | bytes 12582912 | tf_op jit(solution)/shard_map/convert_element_type | solution.py:194
  368.9 9.6 %fusion.11.slope_ref = bf16[16,8,32,768]{3,2,1,0:T(8,128)(2,1)} fusion(bf16[16,8,32,768]{3,2,1,0:T(8,128)(2,1)S(1)} %bitcast.51, bf16[16,8,32,768]{3,2,1,0:T(8,128)(2,1)} %bitcast.62), kind=kLoop, calls=%fused_computation.15 | loop fusion | flops 34603008 | bytes 18874368 | tf_op jit(solution)/shard_map/convert_element_type | solution.py:182
  388.9 7.6 %collective-permute-done.17.refs_1_.refs_2_ = bf16[16,32,768]{2,1,0:T(8,128)(2,1)} collective-permute-done((bf16[16,32,768]{2,1,0:T(8,128)(2,1)}, bf16[16,32,768]{2,1,0:T(8,128)(2,1)}, u32[]{:S(2)}, u32[]{:S(2)}) %collective-permute-start.17) | collective-permute-done | bytes 786464 | tf_op jit(solution)/shard_map/ppermute | solution.py:169
  399.0 14.0 %collective-permute-done.18.refs_1_.refs_6_ = bf16[16,32,768]{2,1,0:T(8,128)(2,1)} collective-permute-done((bf16[16,32,768]{2,1,0:T(8,128)(2,1)}, bf16[16,32,768]{2,1,0:T(8,128)(2,1)}, u32[]{:S(2)}, u32[]{:S(2)}) %collective-permute-start.18) | collective-permute-done | bytes 786464 | tf_op jit(solution)/shard_map/ppermute | solution.py:169
  414.9 15.1 %collective-permute-done.19.refs_1_.refs_3_ = bf16[16,32,768]{2,1,0:T(8,128)(2,1)} collective-permute-done((bf16[16,32,768]{2,1,0:T(8,128)(2,1)S(1)}, bf16[16,32,768]{2,1,0:T(8,128)(2,1)}, u32[]{:S(2)}, u32[]{:S(2)}) %collective-permute-start.19) | collective-permute-done | bytes 786464 | tf_op jit(solution)/shard_map/ppermute | solution.py:169
  431.9 47.0 %collective-permute-done.20.refs_1_.refs_7_ = bf16[16,32,768]{2,1,0:T(8,128)(2,1)S(1)} collective-permute-done((bf16[16,32,768]{2,1,0:T(8,128)(2,1)}, bf16[16,32,768]{2,1,0:T(8,128)(2,1)S(1)}, u32[]{:S(2)}, u32[]{:S(2)}) %collective-permute-start.20) | collective-permute-done | bytes 786464 | tf_op jit(solution)/shard_map/ppermute | solution.py:169
  480.3 6.8 %place.5 = bf16[16,8,32,768]{3,2,1,0:T(8,128)(2,1)} custom-call(s32[1]{0:T(128)} %bitcast.1.at_ref.where_ref, bf16[16,32,768]{2,1,0:T(8,128)(2,1)} %pick.45.refs_0_, bf16[16,32,768]{2,1,0:T(8,128)(2,1)} %collective-permute-done.15.refs_1_, bf16[16,32,768]{2,1,0:T(8,128)(2,1)} %collective-permute-done.17.refs_1_.refs_2_, ...), custom_call_target="tpu_custom_call" | custom-call | flops 393216 | bytes 12582912 | tf_op jit(solution)/shard_map/place/pallas_call | solution.py:110
  487.1 4.6 fusion.24
  491.7 4.6 fusion.19.refs_3_
  496.4 7.4 %convolution_convert_fusion = bf16[16,768,256]{1,2,0:T(8,128)(2,1)} fusion(bf16[16,256,768]{2,1,0:T(8,128)(2,1)} %bitcast.90, bf16[256,16,256]{2,0,1:T(8,128)(2,1)S(1)} %copy-done), kind=kOutput, calls=%fused_computation.28 | convolution fusion | flops 1613758464 | bytes 14680064 | tf_op jit(solution)/shard_map/ibk,bid->bkd/dot_general | solution.py:201
  509.7 3.0 collective-permute-start.23
  521.5 5.6 collective-permute-done.26.y_ref
  532.0 28.8 %collective-permute-done.24.y_ref = bf16[16,32,768]{2,1,0:T(8,128)(2,1)} collective-permute-done((bf16[16,32,768]{2,1,0:T(8,128)(2,1)}, bf16[16,32,768]{2,1,0:T(8,128)(2,1)}, u32[]{:S(2)}, u32[]{:S(2)}) %collective-permute-start.24) | collective-permute-done | bytes 786464 | tf_op jit(solution)/shard_map/ppermute | solution.py:169
  565.7 12.6 %collective-permute-done.22.y_ref = bf16[16,32,768]{2,1,0:T(8,128)(2,1)} collective-permute-done((bf16[16,32,768]{2,1,0:T(8,128)(2,1)}, bf16[16,32,768]{2,1,0:T(8,128)(2,1)}, u32[]{:S(2)}, u32[]{:S(2)}) %collective-permute-start.22) | collective-permute-done | bytes 786464 | tf_op jit(solution)/shard_map/ppermute | solution.py:169
  (133 shorter events, 124.1 us)
Async XLA Ops:
  7.2 80.8 %all-gather.3.cloned.1.call-start = ((), (), s32[]{:S(2)}) async-start(), calls=%async_computation.2 | async-start | bytes 2621440 | tf_op jit(solution)/shard_map/all_gather | solution.py:174
  9.2 166.2 %all-gather.5.cloned.1.call-start = ((), (), s32[]{:S(2)}) async-start(), calls=%async_computation.3 | async-start | bytes 1310720 | tf_op jit(solution)/shard_map/all_gather | solution.py:175
  11.6 69.2 %collective-permute-start = (bf16[16,32,768]{2,1,0:T(8,128)(2,1)}, bf16[16,32,768]{2,1,0:T(8,128)(2,1)S(1)}, u32[]{:S(2)}, u32[]{:S(2)}) collective-permute-start(bf16[16,32,768]{2,1,0:T(8,128)(2,1)} %upstream.8.refs_0_), channel_id=1, source_target_pairs={{0,4},{1,5},{2,6},{3,7},{4,0},{5,1},{6,2},{7,3},{8,12},{9,13},{10,... | collective-permute-start | bytes 2359304 | tf_op jit(solution)/shard_map/ppermute | solution.py:169
  14.3 72.2 %collective-permute-start.1 = (bf16[16,32,768]{2,1,0:T(8,128)(2,1)}, bf16[16,32,768]{2,1,0:T(8,128)(2,1)S(1)}, u32[]{:S(2)}, u32[]{:S(2)}) collective-permute-start(bf16[16,32,768]{2,1,0:T(8,128)(2,1)} %upstream.9.refs_0_), channel_id=1, source_target_pairs={{0,1},{1,0},{2,3},{3,2},{4,5},{5,4},{6,7},{7,6},{8,9},{9,8},{10,11... | collective-permute-start | bytes 2359304 | tf_op jit(solution)/shard_map/ppermute | solution.py:169
  18.1 79.7 %collective-permute-start.2 = (bf16[16,32,768]{2,1,0:T(8,128)(2,1)}, bf16[16,32,768]{2,1,0:T(8,128)(2,1)}, u32[]{:S(2)}, u32[]{:S(2)}) collective-permute-start(bf16[16,32,768]{2,1,0:T(8,128)(2,1)} %upstream.10.refs_0_), channel_id=1, source_target_pairs={{0,5},{1,4},{2,7},{3,6},{4,1},{5,0},{6,3},{7,2},{8,13},{9,12},{10,... | collective-permute-start | bytes 2359304 | tf_op jit(solution)/shard_map/ppermute | solution.py:169
  25.4 124.9 %collective-permute-start.5 = (bf16[16,32,768]{2,1,0:T(8,128)(2,1)}, bf16[16,32,768]{2,1,0:T(8,128)(2,1)}, u32[]{:S(2)}, u32[]{:S(2)}) collective-permute-start(bf16[16,32,768]{2,1,0:T(8,128)(2,1)} %upstream.12.refs_0_), channel_id=1, source_target_pairs={{0,6},{1,7},{2,4},{3,5},{4,2},{5,3},{6,0},{7,1},{8,14},{9,15},{10,... | collective-permute-start | bytes 2359304 | tf_op jit(solution)/shard_map/ppermute | solution.py:169
  28.1 75.9 %collective-permute-start.7 = (bf16[16,32,768]{2,1,0:T(8,128)(2,1)}, bf16[16,32,768]{2,1,0:T(8,128)(2,1)}, u32[]{:S(2)}, u32[]{:S(2)}) collective-permute-start(bf16[16,32,768]{2,1,0:T(8,128)(2,1)} %upstream.13.refs_0_), channel_id=1, source_target_pairs={{0,3},{1,2},{2,1},{3,0},{4,7},{5,6},{6,5},{7,4},{8,11},{9,10},{10,... | collective-permute-start | bytes 2359304 | tf_op jit(solution)/shard_map/ppermute | solution.py:169
  31.2 532.1 %reduce-scatter.5.cloned.1.call-start = ((), (), s32[]{:S(2)}) async-start(), calls=%async_computation.5 | async-start | bytes 2621440 | tf_op jit(solution)/shard_map/reduce_scatter | solution.py:210
  80.8 69.4 %collective-permute-start.4 = (bf16[16,32,768]{2,1,0:T(8,128)(2,1)}, bf16[16,32,768]{2,1,0:T(8,128)(2,1)}, u32[]{:S(2)}, u32[]{:S(2)}) collective-permute-start(bf16[16,32,768]{2,1,0:T(8,128)(2,1)} %upstream.11.refs_0_), channel_id=1, source_target_pairs={{0,2},{1,3},{2,0},{3,1},{4,6},{5,7},{6,4},{7,5},{8,10},{9,11},{10,... | collective-permute-start | bytes 2359304 | tf_op jit(solution)/shard_map/ppermute | solution.py:169
  86.5 81.5 %collective-permute-start.8 = (bf16[16,32,768]{2,1,0:T(8,128)(2,1)}, bf16[16,32,768]{2,1,0:T(8,128)(2,1)}, u32[]{:S(2)}, u32[]{:S(2)}) collective-permute-start(bf16[16,32,768]{2,1,0:T(8,128)(2,1)} %upstream.14.refs_0_), channel_id=1, source_target_pairs={{0,7},{1,6},{2,5},{3,4},{4,3},{5,2},{6,1},{7,0},{8,15},{9,14},{10,... | collective-permute-start | bytes 2359304 | tf_op jit(solution)/shard_map/ppermute | solution.py:169
  97.8 106.0 %collective-permute-start.10 = (bf16[16,32,768]{2,1,0:T(8,128)(2,1)}, bf16[16,32,768]{2,1,0:T(8,128)(2,1)S(1)}, u32[]{:S(2)}, u32[]{:S(2)}) collective-permute-start(bf16[16,32,768]{2,1,0:T(8,128)(2,1)} %pick.25.refs_0_), channel_id=1, source_target_pairs={{0,4},{1,5},{2,6},{3,7},{4,0},{5,1},{6,2},{7,3},{8,12},{9,13},{10,... | collective-permute-start | bytes 2359304 | tf_op jit(solution)/shard_map/ppermute | solution.py:169
  104.0 103.6 %collective-permute-start.3 = (bf16[16,32,768]{2,1,0:T(8,128)(2,1)}, bf16[16,32,768]{2,1,0:T(8,128)(2,1)S(1)}, u32[]{:S(2)}, u32[]{:S(2)}) collective-permute-start(bf16[16,32,768]{2,1,0:T(8,128)(2,1)} %pick.26.refs_0_), channel_id=1, source_target_pairs={{0,1},{1,0},{2,3},{3,2},{4,5},{5,4},{6,7},{7,6},{8,9},{9,8},{10,11... | collective-permute-start | bytes 2359304 | tf_op jit(solution)/shard_map/ppermute | solution.py:169
  194.5 36.2 %collective-permute-start.11 = (bf16[16,32,768]{2,1,0:T(8,128)(2,1)}, bf16[16,32,768]{2,1,0:T(8,128)(2,1)S(1)}, u32[]{:S(2)}, u32[]{:S(2)}) collective-permute-start(bf16[16,32,768]{2,1,0:T(8,128)(2,1)} %pick.27.refs_0_), channel_id=1, source_target_pairs={{0,5},{1,4},{2,7},{3,6},{4,1},{5,0},{6,3},{7,2},{8,13},{9,12},{10,... | collective-permute-start | bytes 2359304 | tf_op jit(solution)/shard_map/ppermute | solution.py:169
  196.4 69.5 %collective-permute-start.6 = (bf16[16,32,768]{2,1,0:T(8,128)(2,1)}, bf16[16,32,768]{2,1,0:T(8,128)(2,1)}, u32[]{:S(2)}, u32[]{:S(2)}) collective-permute-start(bf16[16,32,768]{2,1,0:T(8,128)(2,1)} %pick.28.refs_0_), channel_id=1, source_target_pairs={{0,2},{1,3},{2,0},{3,1},{4,6},{5,7},{6,4},{7,5},{8,10},{9,11},{10,... | collective-permute-start | bytes 2359304 | tf_op jit(solution)/shard_map/ppermute | solution.py:169
  200.2 64.1 %collective-permute-start.12 = (bf16[16,32,768]{2,1,0:T(8,128)(2,1)}, bf16[16,32,768]{2,1,0:T(8,128)(2,1)}, u32[]{:S(2)}, u32[]{:S(2)}) collective-permute-start(bf16[16,32,768]{2,1,0:T(8,128)(2,1)} %pick.29.refs_0_), channel_id=1, source_target_pairs={{0,6},{1,7},{2,4},{3,5},{4,2},{5,3},{6,0},{7,1},{8,14},{9,15},{10,... | collective-permute-start | bytes 2359304 | tf_op jit(solution)/shard_map/ppermute | solution.py:169
  203.8 63.6 %collective-permute-start.9 = (bf16[16,32,768]{2,1,0:T(8,128)(2,1)}, bf16[16,32,768]{2,1,0:T(8,128)(2,1)}, u32[]{:S(2)}, u32[]{:S(2)}) collective-permute-start(bf16[16,32,768]{2,1,0:T(8,128)(2,1)} %pick.30.refs_0_), channel_id=1, source_target_pairs={{0,3},{1,2},{2,1},{3,0},{4,7},{5,6},{6,5},{7,4},{8,11},{9,10},{10,... | collective-permute-start | bytes 2359304 | tf_op jit(solution)/shard_map/ppermute | solution.py:169
  207.5 107.3 %collective-permute-start.13 = (bf16[16,32,768]{2,1,0:T(8,128)(2,1)}, bf16[16,32,768]{2,1,0:T(8,128)(2,1)S(1)}, u32[]{:S(2)}, u32[]{:S(2)}) collective-permute-start(bf16[16,32,768]{2,1,0:T(8,128)(2,1)} %pick.31.refs_0_), channel_id=1, source_target_pairs={{0,7},{1,6},{2,5},{3,4},{4,3},{5,2},{6,1},{7,0},{8,15},{9,14},{10,... | collective-permute-start | bytes 2359304 | tf_op jit(solution)/shard_map/ppermute | solution.py:169
  231.6 132.6 %collective-permute-start.14 = (bf16[16,32,768]{2,1,0:T(8,128)(2,1)}, bf16[16,32,768]{2,1,0:T(8,128)(2,1)S(1)}, u32[]{:S(2)}, u32[]{:S(2)}) collective-permute-start(bf16[16,32,768]{2,1,0:T(8,128)(2,1)} %pick.32.refs_0_), channel_id=1, source_target_pairs={{0,4},{1,5},{2,6},{3,7},{4,0},{5,1},{6,2},{7,3},{8,12},{9,13},{10,... | collective-permute-start | bytes 2359304 | tf_op jit(solution)/shard_map/ppermute | solution.py:169
  264.4 102.8 %collective-permute-start.15 = (bf16[16,32,768]{2,1,0:T(8,128)(2,1)}, bf16[16,32,768]{2,1,0:T(8,128)(2,1)}, u32[]{:S(2)}, u32[]{:S(2)}) collective-permute-start(bf16[16,32,768]{2,1,0:T(8,128)(2,1)} %pick.33.refs_0_), channel_id=1, source_target_pairs={{0,1},{1,0},{2,3},{3,2},{4,5},{5,4},{6,7},{7,6},{8,9},{9,8},{10,11... | collective-permute-start | bytes 2359304 | tf_op jit(solution)/shard_map/ppermute | solution.py:169
  337.5 225.8 %reduce-scatter.3.cloned.1.call-start = ((), (), s32[]{:S(2)}) async-start(), calls=%async_computation.4 | async-start | bytes 5242880 | tf_op jit(solution)/shard_map/reduce_scatter | solution.py:217
  339.6 44.6 %collective-permute-start.16 = (bf16[16,32,768]{2,1,0:T(8,128)(2,1)}, bf16[16,32,768]{2,1,0:T(8,128)(2,1)}, u32[]{:S(2)}, u32[]{:S(2)}) collective-permute-start(bf16[16,32,768]{2,1,0:T(8,128)(2,1)} %pick.34.refs_0_), channel_id=1, source_target_pairs={{0,5},{1,4},{2,7},{3,6},{4,1},{5,0},{6,3},{7,2},{8,13},{9,12},{10,... | collective-permute-start | bytes 2359304 | tf_op jit(solution)/shard_map/ppermute | solution.py:169
  341.6 54.9 %collective-permute-start.17 = (bf16[16,32,768]{2,1,0:T(8,128)(2,1)}, bf16[16,32,768]{2,1,0:T(8,128)(2,1)}, u32[]{:S(2)}, u32[]{:S(2)}) collective-permute-start(bf16[16,32,768]{2,1,0:T(8,128)(2,1)} %pick.35.refs_0_), channel_id=1, source_target_pairs={{0,2},{1,3},{2,0},{3,1},{4,6},{5,7},{6,4},{7,5},{8,10},{9,11},{10,... | collective-permute-start | bytes 2359304 | tf_op jit(solution)/shard_map/ppermute | solution.py:169
  347.0 65.9 %collective-permute-start.18 = (bf16[16,32,768]{2,1,0:T(8,128)(2,1)}, bf16[16,32,768]{2,1,0:T(8,128)(2,1)}, u32[]{:S(2)}, u32[]{:S(2)}) collective-permute-start(bf16[16,32,768]{2,1,0:T(8,128)(2,1)} %pick.36.refs_0_), channel_id=1, source_target_pairs={{0,6},{1,7},{2,4},{3,5},{4,2},{5,3},{6,0},{7,1},{8,14},{9,15},{10,... | collective-permute-start | bytes 2359304 | tf_op jit(solution)/shard_map/ppermute | solution.py:169
  364.2 65.8 %collective-permute-start.19 = (bf16[16,32,768]{2,1,0:T(8,128)(2,1)S(1)}, bf16[16,32,768]{2,1,0:T(8,128)(2,1)}, u32[]{:S(2)}, u32[]{:S(2)}) collective-permute-start(bf16[16,32,768]{2,1,0:T(8,128)(2,1)S(1)} %copy-done.5), channel_id=1, source_target_pairs={{0,3},{1,2},{2,1},{3,0},{4,7},{5,6},{6,5},{7,4},{8,11},{9,10},{10,... | collective-permute-start | bytes 2359304 | tf_op jit(solution)/shard_map/ppermute | solution.py:169
  367.1 111.7 %collective-permute-start.20 = (bf16[16,32,768]{2,1,0:T(8,128)(2,1)}, bf16[16,32,768]{2,1,0:T(8,128)(2,1)S(1)}, u32[]{:S(2)}, u32[]{:S(2)}) collective-permute-start(bf16[16,32,768]{2,1,0:T(8,128)(2,1)} %pick.38.refs_0_), channel_id=1, source_target_pairs={{0,7},{1,6},{2,5},{3,4},{4,3},{5,2},{6,1},{7,0},{8,15},{9,14},{10,... | collective-permute-start | bytes 2359304 | tf_op jit(solution)/shard_map/ppermute | solution.py:169
  384.3 125.4 %collective-permute-start.21 = (bf16[16,32,768]{2,1,0:T(8,128)(2,1)}, bf16[16,32,768]{2,1,0:T(8,128)(2,1)}, u32[]{:S(2)}, u32[]{:S(2)}) collective-permute-start(bf16[16,32,768]{2,1,0:T(8,128)(2,1)} %pick.39.refs_0_), channel_id=1, source_target_pairs={{0,4},{1,5},{2,6},{3,7},{4,0},{5,1},{6,2},{7,3},{8,12},{9,13},{10,... | collective-permute-start | bytes 2359304 | tf_op jit(solution)/shard_map/ppermute | solution.py:169
  396.5 120.5 %collective-permute-start.27 = (bf16[16,32,768]{2,1,0:T(8,128)(2,1)}, bf16[16,32,768]{2,1,0:T(8,128)(2,1)}, u32[]{:S(2)}, u32[]{:S(2)}) collective-permute-start(bf16[16,32,768]{2,1,0:T(8,128)(2,1)} %pick.40.refs_0_), channel_id=1, source_target_pairs={{0,1},{1,0},{2,3},{3,2},{4,5},{5,4},{6,7},{7,6},{8,9},{9,8},{10,11... | collective-permute-start | bytes 2359304 | tf_op jit(solution)/shard_map/ppermute | solution.py:169
  413.0 114.2 %collective-permute-start.26 = (bf16[16,32,768]{2,1,0:T(8,128)(2,1)}, bf16[16,32,768]{2,1,0:T(8,128)(2,1)}, u32[]{:S(2)}, u32[]{:S(2)}) collective-permute-start(bf16[16,32,768]{2,1,0:T(8,128)(2,1)} %pick.41.refs_0_), channel_id=1, source_target_pairs={{0,5},{1,4},{2,7},{3,6},{4,1},{5,0},{6,3},{7,2},{8,13},{9,12},{10,... | collective-permute-start | bytes 2359304 | tf_op jit(solution)/shard_map/ppermute | solution.py:169
  430.0 99.6 %collective-permute-start.25 = (bf16[16,32,768]{2,1,0:T(8,128)(2,1)}, bf16[16,32,768]{2,1,0:T(8,128)(2,1)}, u32[]{:S(2)}, u32[]{:S(2)}) collective-permute-start(bf16[16,32,768]{2,1,0:T(8,128)(2,1)} %pick.42.refs_0_), channel_id=1, source_target_pairs={{0,2},{1,3},{2,0},{3,1},{4,6},{5,7},{6,4},{7,5},{8,10},{9,11},{10,... | collective-permute-start | bytes 2359304 | tf_op jit(solution)/shard_map/ppermute | solution.py:169
  478.8 82.0 %collective-permute-start.24 = (bf16[16,32,768]{2,1,0:T(8,128)(2,1)}, bf16[16,32,768]{2,1,0:T(8,128)(2,1)}, u32[]{:S(2)}, u32[]{:S(2)}) collective-permute-start(bf16[16,32,768]{2,1,0:T(8,128)(2,1)} %pick.43.refs_0_), channel_id=1, source_target_pairs={{0,6},{1,7},{2,4},{3,5},{4,2},{5,3},{6,0},{7,1},{8,14},{9,15},{10,... | collective-permute-start | bytes 2359304 | tf_op jit(solution)/shard_map/ppermute | solution.py:169
  509.7 53.6 %collective-permute-start.23 = (bf16[16,32,768]{2,1,0:T(8,128)(2,1)}, bf16[16,32,768]{2,1,0:T(8,128)(2,1)}, u32[]{:S(2)}, u32[]{:S(2)}) collective-permute-start(bf16[16,32,768]{2,1,0:T(8,128)(2,1)} %pick.44.refs_0_), channel_id=1, source_target_pairs={{0,3},{1,2},{2,1},{3,0},{4,7},{5,6},{6,5},{7,4},{8,11},{9,10},{10,... | collective-permute-start | bytes 2359304 | tf_op jit(solution)/shard_map/ppermute | solution.py:169
  517.0 61.3 %collective-permute-start.22 = (bf16[16,32,768]{2,1,0:T(8,128)(2,1)}, bf16[16,32,768]{2,1,0:T(8,128)(2,1)}, u32[]{:S(2)}, u32[]{:S(2)}) collective-permute-start(bf16[16,32,768]{2,1,0:T(8,128)(2,1)} %pick.46), channel_id=1, source_target_pairs={{0,7},{1,6},{2,5},{3,4},{4,3},{5,2},{6,1},{7,0},{8,15},{9,14},{10,... | collective-permute-start | bytes 2359304 | tf_op jit(solution)/shard_map/ppermute | solution.py:169
  (18 other events, 233.8 us)
Sparse Core Ops, SparseCore 0:
  10.1 22.6 all-gather.2
  34.4 16.7 all-gather.4
  337.6 30.5 reduce-scatter.4
  496.5 44.4 reduce-scatter.2
